TPU v7x, 128 devices: a whole 4x4x4 slice. The times are simulated.
128 devices in a mesh: slab: 8 (over y_lo, x), sector: 16 (over y_hi, z, core).
Axes of the slice: x: 4, y: 4 (y_hi: 2, y_lo: 2; y = y_hi * 2 + y_lo), z: 4, core: 2. Of those that a mesh axis runs over, the one named last changes fastest.
Arguments:
- velocity: float32 [3, 128, 1024, 768], P(None, 'slab', 'sector'), may hold values from -4 to 4
- pressure: float32 [128, 1024, 768], P('slab', 'sector'), may hold values from -4 to 4
- disk_cell: int32 [8, 8192], P('slab', 'sector'), may hold values from 0 to 786431, as said below
- disk_count: int32 [8, 16], P('slab', 'sector'), may hold values from 256 to 512, as said below
- disk_owner: int32 [8, 8192, 1], P('slab', 'sector'), may hold values from 0 to 15; in each aligned block of 512 rows (0 to 511, 512 to 1023, ..., all dimensions but the last counted through in order) at most 48 rows name the same one
- disk_section: int32 [8, 8192], P('slab', 'sector'), may hold values from 0 to 63
- polar: float32 [2, 1024, 256], P(None, 'sector'), may hold values from -1 to 1.5
- geometry: float32 [2, 1024], P(None, 'sector'), may hold values from 0.02 to 0.2
Outputs:
- corrected: float32 [3, 128, 1024, 768], P(None, 'slab', 'sector')
- settled: float32 [128, 1024, 768], P('slab', 'sector')
- section_loads: float32 [2, 1024], P(None, 'sector')
Inputs may be any that keep to these rules, and one draw needn't show every extreme that they name: `disk_cell`: within one device's slots the cells are distinct. `disk_count`: some device uses all 512 slots. `disk_owner`: among the slots of one device at most 48 name the same owner, and exactly 48 do on some device.
All inputs are finite; a program needn't handle non-finite values.
Results may differ from a plain program's by a relative error of at most 0.0003.
Values sent between devices are 32-bit elements; how exact they have to be, the bound alone decides.
A program may use at most 192 MiB of HBM per device.

v0:
```python
import jax
import jax.numpy as jnp
from jax import lax
from jax.sharding import PartitionSpec as P

viscous = 0.1
pressure_step = 0.5
inflow = 1.0
rotation = 10.0
forcing = 0.2
alpha_span = 2.0


def extended_2(cells, sides, width):
    for axis, dim in sides:
        count = lax.axis_size(axis)
        head = lax.slice_in_dim(cells, 0, width, axis=dim)
        tail = lax.slice_in_dim(cells, cells.shape[dim] - width, cells.shape[dim], axis=dim)
        cells = jnp.concatenate(
            [
                lax.ppermute(tail, axis, [(i, (i + 1) % count) for i in range(count)]),
                cells,
                lax.ppermute(head, axis, [((i + 1) % count, i) for i in range(count)]),
            ],
            axis=dim,
        )
    return cells


def ghost_mask(extended, halo_width, dim_pos):
    row_count = extended.shape[dim_pos] - 2 * halo_width
    places = (
        lax.axis_index("slab") * row_count
        - halo_width
        + jnp.arange(row_count + 2 * halo_width, dtype=jnp.int32)
    )
    kept = ((places >= 0) & (places < row_count * lax.axis_size("slab"))).astype(jnp.float32)
    mask_shape = [1] * extended.ndim
    mask_shape[dim_pos] = row_count + 2 * halo_width
    return extended * kept.reshape(mask_shape)


def window(extended, halo_width, region_pad, step_x, step_y):
    dim_x = extended.ndim - 3
    count_x = extended.shape[dim_x] - 2 * halo_width
    count_y = extended.shape[dim_x + 1] - 2 * halo_width
    start_x = halo_width - region_pad + step_x
    start_y = halo_width - region_pad + step_y
    partway = lax.slice_in_dim(extended, start_x, start_x + count_x + 2 * region_pad, axis=dim_x)
    return lax.slice_in_dim(partway, start_y, start_y + count_y + 2 * region_pad, axis=dim_x + 1)


def shift_depth(values, offset):
    widths = [(0, 0)] * values.ndim
    widths[-1] = (1, 1)
    padded = jnp.pad(values, widths)
    length_here = values.shape[-1]
    return lax.slice_in_dim(padded, 1 + offset, 1 + offset + length_here, axis=values.ndim - 1)


def neighbours(extended, halo_width, region_pad):
    centre = window(extended, halo_width, region_pad, 0, 0)
    beside_all = window(extended, halo_width, region_pad, 1, 0) + window(
        extended, halo_width, region_pad, -1, 0
    )
    beside_all = (
        beside_all
        + window(extended, halo_width, region_pad, 0, 1)
        + window(extended, halo_width, region_pad, 0, -1)
    )
    beside_all = beside_all + shift_depth(centre, 1) + shift_depth(centre, -1)
    return (beside_all, centre)


def gradient_from(extended, halo_width, region_pad):
    centre = window(extended, halo_width, region_pad, 0, 0)
    along_x = 0.5 * (
        window(extended, halo_width, region_pad, 1, 0)
        - window(extended, halo_width, region_pad, -1, 0)
    )
    along_y = 0.5 * (
        window(extended, halo_width, region_pad, 0, 1)
        - window(extended, halo_width, region_pad, 0, -1)
    )
    along_z = 0.5 * (shift_depth(centre, 1) - shift_depth(centre, -1))
    return jnp.stack([along_x, along_y, along_z])


def divergence_from(extended, halo_width, region_pad):
    along_x = 0.5 * (
        window(extended[0], halo_width, region_pad, 1, 0)
        - window(extended[0], halo_width, region_pad, -1, 0)
    )
    along_y = 0.5 * (
        window(extended[1], halo_width, region_pad, 0, 1)
        - window(extended[1], halo_width, region_pad, 0, -1)
    )
    centre = window(extended[2], halo_width, region_pad, 0, 0)
    along_z = 0.5 * (shift_depth(centre, 1) - shift_depth(centre, -1))
    return along_x + along_y + along_z


def blade_forces(
    axial_part, turning, radius, chord_len, twist_ang, lift_rows, drag_rows, bin_total
):
    axial_speed = inflow + axial_part
    tangent_speed = rotation * radius + turning
    inflow_angle = jnp.arctan2(axial_speed, tangent_speed)
    position = (inflow_angle - twist_ang + alpha_span) * ((bin_total - 1) / (2.0 * alpha_span))
    bin_ids = jnp.arange(bin_total, dtype=jnp.float32)
    weights = jnp.maximum(0.0, 1.0 - jnp.abs(position[..., None] - bin_ids))
    lift_coef = jnp.sum(lift_rows * weights, -1)
    drag_coef = jnp.sum(drag_rows * weights, -1)
    dynamic = 0.5 * (axial_speed * axial_speed + tangent_speed * tangent_speed) * chord_len
    cosine = jnp.cos(inflow_angle)
    sine = jnp.sin(inflow_angle)
    thrust = dynamic * (lift_coef * cosine - drag_coef * sine)
    swirl_force = dynamic * (lift_coef * sine + drag_coef * cosine)
    return (thrust, swirl_force)


def on_device(velocity, pressure, disk_cell, disk_count, disk_owner, disk_section, polar, geometry):
    size_x, size_y, size_z = pressure.shape
    highest = lax.Precision.HIGHEST
    first_ext = extended_2(
        jnp.concatenate([velocity, pressure[None]], 0), (("slab", 1), ("sector", 2)), 1
    )
    first_ext = ghost_mask(first_ext, 1, 1)
    beside_all, centre = neighbours(first_ext[:3], 1, 0)
    predicted = (
        centre
        + viscous * (beside_all - 6.0 * centre)
        - pressure_step * gradient_from(first_ext[3], 1, 0)
    )
    slot_count = disk_cell.shape[1]
    cell_ids = disk_cell[0]
    active = jnp.arange(slot_count, dtype=jnp.int32) < disk_count[0, 0]
    owner_ids = disk_owner[0, :, 0]
    local_section = disk_section[0]
    flat_flow = predicted.reshape(3, size_x * size_y * size_z)
    axial_part = flat_flow[0, cell_ids]
    turning = flat_flow[1, cell_ids]
    radius = 0.25 + 0.75 * ((cell_ids % size_z).astype(jnp.float32) + 0.5) / size_z
    sec_dev = polar.shape[1]
    angles = polar.shape[2]
    owner_count = lax.axis_size("sector")
    capacity = max(2, 3 * slot_count // (2 * owner_count))
    chosen = (
        (owner_ids[:, None] == jnp.arange(owner_count, dtype=jnp.int32)[None, :]) & active[:, None]
    ).astype(jnp.int32)
    rank_in = jnp.sum((jnp.cumsum(chosen, 0) - chosen) * chosen, 1)
    target = jnp.where(active, owner_ids, owner_count)
    payload = jnp.stack([axial_part, turning, radius, local_section.astype(jnp.float32)], 1)
    outbox = jnp.zeros((owner_count, 4, capacity), jnp.float32).at[:, 3, :].set(-1.0)
    outbox = outbox.at[target, :, rank_in].set(payload, mode="drop")
    arrived = lax.all_to_all(outbox, "sector", split_axis=0, concat_axis=0, tiled=True)
    one_hot = (arrived[:, 3, :][..., None] == jnp.arange(sec_dev, dtype=jnp.float32)).astype(
        jnp.float32
    )
    chord_len = jnp.einsum("ncs,s->nc", one_hot, geometry[0], precision=highest)
    twist_ang = jnp.einsum("ncs,s->nc", one_hot, geometry[1], precision=highest)
    lift_rows = jnp.einsum("ncs,sa->nca", one_hot, polar[0], precision=highest)
    drag_rows = jnp.einsum("ncs,sa->nca", one_hot, polar[1], precision=highest)
    thrust, swirl_force = blade_forces(
        arrived[:, 0, :],
        arrived[:, 1, :],
        arrived[:, 2, :],
        chord_len,
        twist_ang,
        lift_rows,
        drag_rows,
        angles,
    )
    result = jnp.stack([thrust, swirl_force, swirl_force * arrived[:, 2, :], arrived[:, 3, :]], 1)
    answer = lax.all_to_all(result[:, :2, :], "sector", split_axis=0, concat_axis=0, tiled=True)
    home_row = jnp.minimum(target, owner_count - 1)
    returned = answer[home_row, :, rank_in]
    thrust = jnp.where(active, returned[:, 0], 0.0)
    swirl_force = jnp.where(active, returned[:, 1], 0.0)
    one_hot = (result[:, 3, :][..., None] == jnp.arange(sec_dev, dtype=jnp.float32)).astype(
        jnp.float32
    )
    partial_value = jnp.stack(
        [
            jnp.einsum("ncs,nc->s", one_hot, result[:, 0, :], precision=highest),
            jnp.einsum("ncs,nc->s", one_hot, result[:, 2, :], precision=highest),
        ]
    )
    section_loads = lax.psum(partial_value, "slab")
    flat_flow = flat_flow.at[0, cell_ids].add(forcing * thrust)
    flat_flow = flat_flow.at[1, cell_ids].add(forcing * swirl_force)
    pushed = flat_flow.reshape(3, size_x, size_y, size_z)
    second = ghost_mask(extended_2(pushed, (("slab", 1), ("sector", 2)), 1), 1, 1)
    source = divergence_from(second, 1, 0)
    beside_all, centre = neighbours(first_ext[3], 1, 0)
    middle = (beside_all - source) / 6.0
    third_ext = ghost_mask(extended_2(middle, (("slab", 0), ("sector", 1)), 1), 1, 0)
    beside_all, centre = neighbours(third_ext, 1, 0)
    settled = (beside_all - source) / 6.0
    last_ext = ghost_mask(extended_2(settled, (("slab", 0), ("sector", 1)), 1), 1, 0)
    corrected = pushed - gradient_from(last_ext, 1, 0)
    return (corrected, settled, section_loads)


def solution(mesh):
    return jax.shard_map(
        on_device,
        mesh=mesh,
        in_specs=(
            P(None, "slab", "sector", None),
            P("slab", "sector", None),
            P("slab", "sector"),
            P("slab", "sector"),
            P("slab", "sector", None),
            P("slab", "sector"),
            P(None, "sector", None),
            P(None, "sector"),
        ),
        out_specs=(P(None, "slab", "sector", None), P("slab", "sector", None), P(None, "sector")),
        check_vma=False,
    )
```

profile of v0, /device:TPU:0, one launch (start us, length us, event | category | flops | bytes accessed | tf_op | source)
XLA Modules:
  0.0 521.2 jit_solution(15383737262913093529)
XLA Ops:
  0.7 2.8 pad_maximum_fusion.1
  3.5 1.6 collective-permute-start
  5.1 2.6 collective-permute-start.1
  10.0 3.1 reduce-window.6
  13.2 1.0 slice_reduce_fusion.2
  17.2 8.1 %collective-permute-done = f32[4,1,64,768]{3,2,1,0:T(8,128)} collective-permute-done((f32[4,1,64,768]{3,2,1,0:T(8,128)}, f32[4,1,64,768]{3,2,1,0:T(8,128)}, u32[]{:S(2)}, u32[]{:S(2)}) %collective-permute-start) | collective-permute-done | bytes 786464 | tf_op jit(solution)/shard_map/ppermute | solution.py:21
  25.2 2.3 pad_maximum_fusion.5
  27.6 5.7 %collective-permute-start.3 = (f32[4,18,1,768]{3,2,1,0:T(1,128)S(1)}, f32[4,18,1,768]{3,2,1,0:T(1,128)S(1)}, u32[]{:S(2)}, u32[]{:S(2)}) collective-permute-start(f32[4,18,1,768]{3,2,1,0:T(1,128)S(1)} %get-tuple-element.30), channel_id=1, source_target_pairs={{1,0},{2,1},{3,2},{4,3},{5,4},{6,5},{7,6},{8,7},{9,8},{10,9},{11,1... | collective-permute-start | bytes 663560 | tf_op jit(solution)/shard_map/ppermute | solution.py:23
  33.9 2.7 collective-permute-done.2
  36.7 10.4 %maximum_multiply_fusion = f32[4,18,66,768]{3,2,1,0:T(8,128)} fusion(f32[4,18,1,768]{3,2,1,0:T(1,128)S(1)} %collective-permute-done.3, f32[4,1,64,768]{3,2,1,0:T(8,128)} %collective-permute-done.1, f32[1,16,64,768]{3,2,1,0:T(8,128)S(1)} %bitcast.160, f32[3,16,64,768]{3,2,1,0:T(8,128)S(1)} %copy-done.1, f32[4,1,64,768]{3,2,1,0:T(8,128)} %collective-permute-done, ...), kind=kLoop, calls=%fused_computation.6 | loop fusion | flops 21897216 | bytes 29196360 | tf_op jit(solution)/shard_map/mul | solution.py:40
  47.1 5.0 slice_bitcast_fusion.6
  52.2 11.7 %slice.404 = f32[3,16,64,768]{3,2,1,0:T(8,128)} slice(f32[4,18,66,768]{3,2,1,0:T(8,128)} %maximum_multiply_fusion), slice={[0:3], [1:17], [1:65], [0:768]} | slice | bytes 18874368 | tf_op jit(solution)/shard_map/slice | solution.py:50
  64.0 2.6 multiply_bitcast_fusion.1
  66.5 4.9 multiply_bitcast_fusion
  71.4 29.7 %fusion.5 = f32[3,16,64,768]{3,2,1,0:T(8,128)} fusion(f32[3,16,64,768]{3,2,1,0:T(8,128)} %slice.404, f32[4,18,66,768]{3,2,1,0:T(8,128)} %maximum_multiply_fusion, f32[1,16,64,768]{3,2,1,0:T(8,128)} %get-tuple-element.65, f32[1,16,64,768]{3,2,1,0:T(8,128)} %get-tuple-element.48, f32[1,16,64,768]{3,2,1,0:T(8,128)} %get-tuple-element.66), kind=kLoop, calls=%fused_computation.15 | loop fusion | flops 30670848 | bytes 66060288 | tf_op jit(solution)/shard_map/sub | solution.py:131
  101.1 15.0 %copy.49 = f32[1,3,1024,768]{3,1,2,0:T(4,128)} copy(f32[1,3,1024,768]{3,2,1,0:T(8,128)} %bitcast.151) | data formatting | bytes 18874368
  116.1 9.2 %gather_fusion = f32[512]{0:T(512)} fusion(f32[3,786432]{1,0:T(4,128)} %bitcast.147, s32[512]{0:T(512)} %bitcast.157), kind=kCustom, calls=%fused_computation | custom fusion | bytes 8192 | tf_op jit(solution)/shard_map/gather | solution.py:141
  125.4 9.1 %gather_fusion.1 = f32[512]{0:T(512)} fusion(f32[3,786432]{1,0:T(4,128)} %bitcast.148, s32[512]{0:T(512)} %bitcast.156), kind=kCustom, calls=%fused_computation.1 | custom fusion | bytes 8192 | tf_op jit(solution)/shard_map/gather | solution.py:142
  134.5 1.3 pad_maximum_fusion.13
  135.8 1.5 copy.32
  137.4 52.5 %scatter_fusion = f32[16,4,48]{1,2,0:T(8,128)} fusion(f32[16,4,48]{1,2,0:T(8,128)} %copy.59, s32[512]{0:T(512)S(1)} %bitcast.155, f32[512,4]{1,0:T(8,128)} %copy.32), kind=kCustom, calls=%fused_computation.3 | custom fusion | bytes 28672 | tf_op jit(solution)/shard_map/scatter | solution.py:155
  189.8 1.8 copy.33
  191.6 1.5 reshape.279
  193.1 15.4 %all_to_all.10 = f32[16,1,192]{2,1,0:T(1,128)} all-to-all(f32[16,1,192]{2,1,0:T(1,128)} %reshape.279), channel_id=1, replica_groups=mesh['slab'=8,'sector'=16] {'sector'}, dimensions={0} | all-to-all | bytes 24576 | tf_op jit(solution)/shard_map/all_to_all | solution.py:156
  209.0 2.0 reduce.8
  211.0 1.4 reshape.280
  212.4 0.9 fusion.60
  213.4 1.4 fusion.23
  214.9 1.4 fusion.21
  216.4 1.5 fusion.22
  217.8 1.4 fusion.24
  220.5 10.8 %all_to_all.11 = f32[16,2,48]{2,1,0:T(2,128)} all-to-all(f32[16,2,48]{2,1,0:T(2,128)S(1)} %copy.38), channel_id=1, replica_groups=mesh['slab'=8,'sector'=16] {'sector'}, dimensions={0} | all-to-all | bytes 12288 | tf_op jit(solution)/shard_map/all_to_all | solution.py:175
  231.3 1.7 copy.39
  233.0 5.4 %gather_fusion.2 = f32[512,2]{1,0:T(8,128)} fusion(f32[16,2,48]{1,2,0:T(8,128)} %copy.39, s32[512]{0:T(512)S(1)} %bitcast.154), kind=kCustom, calls=%fused_computation.2 | custom fusion | bytes 12288 | tf_op jit(solution)/shard_map/gather | solution.py:177
  238.4 1.3 slice_reduce_fusion
  239.7 59.7 %scatter_fusion.1 = f32[3,786432]{1,0:T(4,128)} fusion(f32[3,786432]{1,0:T(4,128)} %bitcast.149, s32[512]{0:T(512)S(1)} %bitcast.153, f32[512]{0:T(512)S(1)} %select_multiply_fusion.1), kind=kCustom, calls=%fused_computation.4 | custom fusion | flops 512 | bytes 10240 | tf_op jit(solution)/shard_map/scatter-add | solution.py:190
  299.4 59.7 %scatter_fusion.2 = f32[3,786432]{1,0:T(4,128)} fusion(f32[3,786432]{1,0:T(4,128)} %scatter_fusion.1, s32[512]{0:T(512)S(1)} %bitcast.152, f32[512]{0:T(512)S(1)} %select_multiply_fusion), kind=kCustom, calls=%fused_computation.5 | custom fusion | flops 512 | bytes 10240 | tf_op jit(solution)/shard_map/scatter-add | solution.py:191
  359.1 6.4 %copy.50 = f32[1,3,1024,768]{3,2,1,0:T(8,128)S(1)} copy(f32[1,3,1024,768]{3,1,2,0:T(4,128)} %bitcast.150) | data formatting | bytes 18874368
  365.7 4.1 collective-permute-start.5
  369.8 13.3 %collective-permute-done.4 = f32[3,1,64,768]{3,2,1,0:T(8,128)S(1)} collective-permute-done((f32[3,1,64,768]{3,2,1,0:T(8,128)S(1)}, f32[3,1,64,768]{3,2,1,0:T(8,128)S(1)}, u32[]{:S(2)}, u32[]{:S(2)}) %collective-permute-start.4) | collective-permute-done | bytes 589856 | tf_op jit(solution)/shard_map/ppermute | solution.py:21
  383.2 0.9 constant_dynamic-update-slice_fusion.2
  384.1 4.6 constant_dynamic-update-slice_fusion.1
  388.7 0.9 constant_dynamic-update-slice_fusion
  389.6 2.0 fusion.56
  391.6 5.3 %collective-permute-start.7 = (f32[3,18,1,768]{3,2,1,0:T(1,128)S(1)}, f32[3,18,1,768]{3,2,1,0:T(1,128)S(1)}, u32[]{:S(2)}, u32[]{:S(2)}) collective-permute-start(f32[3,18,1,768]{3,2,1,0:T(1,128)S(1)} %get-tuple-element.38), channel_id=1, source_target_pairs={{1,0},{2,1},{3,2},{4,3},{5,4},{6,5},{7,6},{8,7},{9,8},{10,9},{11,1... | collective-permute-start | bytes 497672 | tf_op jit(solution)/shard_map/ppermute | solution.py:23
  397.0 3.0 collective-permute-done.6
  400.0 10.0 %maximum_multiply_fusion.1 = f32[3,18,66,768]{3,2,1,0:T(8,128)} fusion(f32[3,18,1,768]{3,2,1,0:T(1,128)S(1)} %collective-permute-done.7, f32[3,18,64,768]{3,2,1,0:T(8,128)} %constant_dynamic-update-slice_fusion, f32[3,18,1,768]{3,2,1,0:T(1,128)S(1)} %collective-permute-done.6, f32[18]{0:T(128)S(1)} %copy-done.15), kind=kLoop, calls=%fused_computation.7 | loop fusion | flops 8211456 | bytes 21897288 | tf_op jit(solution)/shard_map/mul | solution.py:40
  410.0 10.3 %slice_bitcast_fusion.3 = (f32[16,66,768]{2,1,0:T(8,128)}, f32[16,66,768]{2,1,0:T(8,128)}, f32[16,66,768]{2,1,0:T(8,128)}, f32[16,66,768]{2,1,0:T(8,128)}) fusion(f32[3,18,66,768]{3,2,1,0:T(8,128)} %maximum_multiply_fusion.1), kind=kLoop, calls=%fused_computation.34 | loop fusion | bytes 25952256 | tf_op jit(solution)/shard_map/slice | solution.py:49
  420.3 4.0 slice.436
  424.4 14.4 %subtract_multiply_fusion = (f32[16,64,768]{2,1,0:T(8,128)S(1)}, f32[16,64,768]{2,1,0:T(8,128)}) fusion(f32[16,66,768]{2,1,0:T(8,128)S(1)} %get-tuple-element.27, f32[16,66,768]{2,1,0:T(8,128)} %copy-done.6, f32[16,66,768]{2,1,0:T(8,128)} %copy-done.5, f32[16,64,768]{2,1,0:T(8,128)} %copy-done.4, f32[16,64,768]{2,1,0:T(8,128)} %slice.436, ...), kind=kLoop, calls=%fused_computation.60 | loop fusion | flops 10223616 | bytes 37748736 | tf_op jit(solution)/shard_map/div | solution.py:196
  438.8 4.1 collective-permute-start.9
  443.0 3.6 collective-permute-done.8
  446.8 5.3 %collective-permute-start.11 = (f32[18,1,768]{2,1,0:T(1,128)S(1)}, f32[18,1,768]{2,1,0:T(1,128)S(1)}, u32[]{:S(2)}, u32[]{:S(2)}) collective-permute-start(f32[18,1,768]{2,1,0:T(1,128)S(1)} %get-tuple-element.47), channel_id=1, source_target_pairs={{1,0},{2,1},{3,2},{4,3},{5,4},{6,5},{7,6},{8,7},{9,8},{10,9},{11,1... | collective-permute-start | bytes 165896 | tf_op jit(solution)/shard_map/ppermute | solution.py:23
  452.1 1.8 collective-permute-done.10
  454.9 1.5 copy-done.9
  456.4 2.3 fusion.12
  458.8 4.2 collective-permute-start.13
  463.7 2.9 collective-permute-done.12
  467.3 5.4 %collective-permute-start.15 = (f32[18,1,768]{2,1,0:T(1,128)}, f32[18,1,768]{2,1,0:T(1,128)}, u32[]{:S(2)}, u32[]{:S(2)}) collective-permute-start(f32[18,1,768]{2,1,0:T(1,128)} %get-tuple-element.45), channel_id=1, source_target_pairs={{1,0},{2,1},{3,2},{4,3},{5,4},{6,5},{7,6},{8,7},{9,8},{10,9},{11,1... | collective-permute-start | bytes 165896 | tf_op jit(solution)/shard_map/ppermute | solution.py:23
  472.7 20.9 %psum.7 = f32[2,64]{1,0:T(2,128)} all-reduce(f32[2,64]{1,0:T(2,128)S(1)} %pad_maximum_fusion.14), channel_id=1, replica_groups=mesh['slab'=8,'sector'=16] {'slab'}, use_global_device_ids=true, to_apply=%region_8.9 | all-reduce | flops 128 | bytes 1024 | tf_op jit(solution)/shard_map/psum | solution.py:189
  493.6 3.2 maximum_multiply_fusion.4
  496.8 10.6 %fusion.19 = (f32[1,16,64,768]{3,2,1,0:T(8,128)}, f32[16,64,768]{2,1,0:T(8,128)}, f32[1,16,64,768]{3,2,1,0:T(8,128)}) fusion(f32[18,66,768]{2,1,0:T(8,128)} %maximum_multiply_fusion.4), kind=kLoop, calls=%fused_computation.53 | loop fusion | flops 3145728 | bytes 25165824 | tf_op jit(solution)/shard_map/stack | solution.py:86
  507.4 4.7 fusion.15
  512.1 8.9 %maximum_subtract_fusion = f32[3,16,64,768]{3,2,1,0:T(8,128)} fusion(f32[3,16,64,768]{3,2,1,0:T(8,128)} %bitcast.146, f32[1,16,64,768]{3,2,1,0:T(8,128)S(1)} %fusion.15, f32[1,16,64,768]{3,2,1,0:T(8,128)S(1)} %copy-done.8, f32[1,16,64,768]{3,2,1,0:T(8,128)S(1)} %copy-done.7), kind=kLoop, calls=%fused_computation.20 | loop fusion | flops 7077888 | bytes 28311552 | tf_op jit(solution)/shard_map/sub | solution.py:201
  (89 shorter events, 10.4 us)
Async XLA Ops:
  0.6 7.5 %copy-start.16 = (s32[1,512]{1,0:T(1,128)S(1)}, s32[1,512]{1,0:T(1,128)}, u32[]{:S(2)}) copy-start(s32[1,512]{1,0:T(1,128)} %param.12) | copy-start | bytes 6148
  0.6 8.8 %copy-start.13 = (s32[1,512,1]{1,2,0:T(1,128)S(1)}, s32[1,512,1]{1,2,0:T(1,128)}, u32[]{:S(2)}) copy-start(s32[1,512,1]{1,2,0:T(1,128)} %param.14) | copy-start | bytes 6148
  0.7 13.5 %copy-start.10 = (f32[16,4,48]{1,2,0:T(8,128)S(1)}, f32[16,4,48]{1,2,0:T(8,128)}, u32[]{:S(2)}) copy-start(f32[16,4,48]{1,2,0:T(8,128)} %constant.96.clone.1) | copy-start | bytes 36868
  0.7 24.6 %copy-start.3 = (f32[16,64,768]{2,1,0:T(8,128)S(1)}, f32[16,64,768]{2,1,0:T(8,128)}, u32[]{:S(2)}) copy-start(f32[16,64,768]{2,1,0:T(8,128)} %param.11) | copy-start | bytes 9437188
  3.5 21.7 %collective-permute-start = (f32[4,1,64,768]{3,2,1,0:T(8,128)}, f32[4,1,64,768]{3,2,1,0:T(8,128)}, u32[]{:S(2)}, u32[]{:S(2)}) collective-permute-start(f32[4,1,64,768]{3,2,1,0:T(8,128)} %get-tuple-element.31), channel_id=1, source_target_pairs={{0,16},{16,32},{32,48},{48,64},{64,80},{80,96},{96,112},{112,0},{1... | collective-permute-start | bytes 2359304 | tf_op jit(solution)/shard_map/ppermute | solution.py:21
  5.1 20.1 %collective-permute-start.1 = (f32[4,1,64,768]{3,2,1,0:T(8,128)}, f32[4,1,64,768]{3,2,1,0:T(8,128)}, u32[]{:S(2)}, u32[]{:S(2)}) collective-permute-start(f32[4,1,64,768]{3,2,1,0:T(8,128)} %get-tuple-element.32), channel_id=1, source_target_pairs={{16,0},{32,16},{48,32},{64,48},{80,64},{96,80},{112,96},{0,112},{1... | collective-permute-start | bytes 2359304 | tf_op jit(solution)/shard_map/ppermute | solution.py:23
  17.1 16.1 %copy-start.20 = (s32[1,512]{1,0:T(1,128)S(1)}, s32[1,512]{1,0:T(1,128)}, u32[]{:S(2)}) copy-start(s32[1,512]{1,0:T(1,128)} %param.15) | copy-start | bytes 6148
  17.1 19.6 %copy-start.14 = (f32[18]{0:T(128)S(1)}, f32[18]{0:T(128)}, u32[]{:S(2)}) copy-start(f32[18]{0:T(128)} %and_convert_fusion) | copy-start | bytes 220
  25.2 11.5 %copy-start.1 = (f32[3,16,64,768]{3,2,1,0:T(8,128)S(1)}, f32[3,16,64,768]{3,2,1,0:T(8,128)}, u32[]{:S(2)}) copy-start(f32[3,16,64,768]{3,2,1,0:T(8,128)} %param.10) | copy-start | bytes 28311556
  27.5 9.0 %collective-permute-start.2 = (f32[4,18,1,768]{3,2,1,0:T(1,128)S(1)}, f32[4,18,1,768]{3,2,1,0:T(1,128)S(1)}, u32[]{:S(2)}, u32[]{:S(2)}) collective-permute-start(f32[4,18,1,768]{3,2,1,0:T(1,128)S(1)} %get-tuple-element.29), channel_id=1, source_target_pairs={{0,1},{1,2},{2,3},{3,4},{4,5},{5,6},{6,7},{7,8},{8,9},{9,10},{10,1... | collective-permute-start | bytes 663560 | tf_op jit(solution)/shard_map/ppermute | solution.py:21
  27.6 9.1 %collective-permute-start.3 = (f32[4,18,1,768]{3,2,1,0:T(1,128)S(1)}, f32[4,18,1,768]{3,2,1,0:T(1,128)S(1)}, u32[]{:S(2)}, u32[]{:S(2)}) collective-permute-start(f32[4,18,1,768]{3,2,1,0:T(1,128)S(1)} %get-tuple-element.30), channel_id=1, source_target_pairs={{1,0},{2,1},{3,2},{4,3},{5,4},{6,5},{7,6},{8,7},{9,8},{10,9},{11,1... | collective-permute-start | bytes 663560 | tf_op jit(solution)/shard_map/ppermute | solution.py:23
  52.2 14.3 %copy-start.5 = (f32[16,66,768]{2,1,0:T(8,128)}, f32[16,66,768]{2,1,0:T(8,128)S(1)}, u32[]{:S(2)}) copy-start(f32[16,66,768]{2,1,0:T(8,128)S(1)} %get-tuple-element.26) | copy-start | bytes 9732100
  52.2 14.3 %copy-start.6 = (f32[16,66,768]{2,1,0:T(8,128)}, f32[16,66,768]{2,1,0:T(8,128)S(1)}, u32[]{:S(2)}) copy-start(f32[16,66,768]{2,1,0:T(8,128)S(1)} %get-tuple-element.28) | copy-start | bytes 9732100
  66.5 4.9 copy-start.4
  213.3 6.6 %copy-start.17 = (f32[16,1,48]{2,1,0:T(1,128)}, f32[16,1,48]{2,1,0:T(1,128)S(1)}, u32[]{:S(2)}) copy-start(f32[16,1,48]{2,1,0:T(1,128)S(1)} %get-tuple-element.54) | copy-start | bytes 9220
  219.9 0.6 copy-start.11
  365.5 23.2 %copy-start = (f32[1,3,1024,768]{3,2,1,0:T(8,128)}, f32[1,3,1024,768]{3,2,1,0:T(8,128)S(1)}, u32[]{:S(2)}) copy-start(f32[1,3,1024,768]{3,2,1,0:T(8,128)S(1)} %copy.50) | copy-start | bytes 28311556
  365.6 17.5 %collective-permute-start.4 = (f32[3,1,64,768]{3,2,1,0:T(8,128)S(1)}, f32[3,1,64,768]{3,2,1,0:T(8,128)S(1)}, u32[]{:S(2)}, u32[]{:S(2)}) collective-permute-start(f32[3,1,64,768]{3,2,1,0:T(8,128)S(1)} %get-tuple-element.40), channel_id=1, source_target_pairs={{0,16},{16,32},{32,48},{48,64},{64,80},{80,96},{96,112},{112,0},{1... | collective-permute-start | bytes 1769480 | tf_op jit(solution)/shard_map/ppermute | solution.py:21
  365.7 23.0 %collective-permute-start.5 = (f32[3,1,64,768]{3,2,1,0:T(8,128)S(1)}, f32[3,1,64,768]{3,2,1,0:T(8,128)S(1)}, u32[]{:S(2)}, u32[]{:S(2)}) collective-permute-start(f32[3,1,64,768]{3,2,1,0:T(8,128)S(1)} %get-tuple-element.39), channel_id=1, source_target_pairs={{16,0},{32,16},{48,32},{64,48},{80,64},{96,80},{112,96},{0,112},{1... | collective-permute-start | bytes 1769480 | tf_op jit(solution)/shard_map/ppermute | solution.py:23
  384.1 15.9 %copy-start.15 = (f32[18]{0:T(128)S(1)}, f32[18]{0:T(128)}, u32[]{:S(2)}) copy-start(f32[18]{0:T(128)} %and_convert_fusion) | copy-start | bytes 220
  391.5 8.4 %collective-permute-start.6 = (f32[3,18,1,768]{3,2,1,0:T(1,128)S(1)}, f32[3,18,1,768]{3,2,1,0:T(1,128)S(1)}, u32[]{:S(2)}, u32[]{:S(2)}) collective-permute-start(f32[3,18,1,768]{3,2,1,0:T(1,128)S(1)} %get-tuple-element.37), channel_id=1, source_target_pairs={{0,1},{1,2},{2,3},{3,4},{4,5},{5,6},{6,7},{7,8},{8,9},{9,10},{10,1... | collective-permute-start | bytes 497672 | tf_op jit(solution)/shard_map/ppermute | solution.py:21
  391.6 8.4 %collective-permute-start.7 = (f32[3,18,1,768]{3,2,1,0:T(1,128)S(1)}, f32[3,18,1,768]{3,2,1,0:T(1,128)S(1)}, u32[]{:S(2)}, u32[]{:S(2)}) collective-permute-start(f32[3,18,1,768]{3,2,1,0:T(1,128)S(1)} %get-tuple-element.38), channel_id=1, source_target_pairs={{1,0},{2,1},{3,2},{4,3},{5,4},{6,5},{7,6},{8,7},{9,8},{10,9},{11,1... | collective-permute-start | bytes 497672 | tf_op jit(solution)/shard_map/ppermute | solution.py:23
  438.8 7.8 %collective-permute-start.8 = (f32[1,64,768]{2,1,0:T(8,128)S(1)}, f32[1,64,768]{2,1,0:T(8,128)S(1)}, u32[]{:S(2)}, u32[]{:S(2)}) collective-permute-start(f32[1,64,768]{2,1,0:T(8,128)S(1)} %get-tuple-element.52), channel_id=1, source_target_pairs={{0,16},{16,32},{32,48},{48,64},{64,80},{80,96},{96,112},{112,0},{1... | collective-permute-start | bytes 589832 | tf_op jit(solution)/shard_map/ppermute | solution.py:21
  438.8 7.8 %collective-permute-start.9 = (f32[1,64,768]{2,1,0:T(8,128)S(1)}, f32[1,64,768]{2,1,0:T(8,128)S(1)}, u32[]{:S(2)}, u32[]{:S(2)}) collective-permute-start(f32[1,64,768]{2,1,0:T(8,128)S(1)} %get-tuple-element.53), channel_id=1, source_target_pairs={{16,0},{32,16},{48,32},{64,48},{80,64},{96,80},{112,96},{0,112},{1... | collective-permute-start | bytes 589832 | tf_op jit(solution)/shard_map/ppermute | solution.py:23
  446.7 7.3 %collective-permute-start.10 = (f32[18,1,768]{2,1,0:T(1,128)S(1)}, f32[18,1,768]{2,1,0:T(1,128)S(1)}, u32[]{:S(2)}, u32[]{:S(2)}) collective-permute-start(f32[18,1,768]{2,1,0:T(1,128)S(1)} %get-tuple-element.46), channel_id=1, source_target_pairs={{0,1},{1,2},{2,3},{3,4},{4,5},{5,6},{6,7},{7,8},{8,9},{9,10},{10,1... | collective-permute-start | bytes 165896 | tf_op jit(solution)/shard_map/ppermute | solution.py:21
  446.8 7.2 %collective-permute-start.11 = (f32[18,1,768]{2,1,0:T(1,128)S(1)}, f32[18,1,768]{2,1,0:T(1,128)S(1)}, u32[]{:S(2)}, u32[]{:S(2)}) collective-permute-start(f32[18,1,768]{2,1,0:T(1,128)S(1)} %get-tuple-element.47), channel_id=1, source_target_pairs={{1,0},{2,1},{3,2},{4,3},{5,4},{6,5},{7,6},{8,7},{9,8},{10,9},{11,1... | collective-permute-start | bytes 165896 | tf_op jit(solution)/shard_map/ppermute | solution.py:23
  454.5 1.9 copy-start.9
  456.4 6.6 %copy-start.12 = (f32[16,48]{1,0:T(8,128)S(1)}, f32[16,48]{1,0:T(8,128)}, u32[]{:S(2)}) copy-start(f32[16,48]{1,0:T(8,128)} %copy-done.11) | copy-start | bytes 9220
  456.4 6.6 %copy-start.18 = (f32[16,1,48]{2,1,0:T(1,128)S(1)}, f32[16,1,48]{2,1,0:T(1,128)}, u32[]{:S(2)}) copy-start(f32[16,1,48]{2,1,0:T(1,128)} %copy-done.17) | copy-start | bytes 9220
  456.4 7.0 %copy-start.19 = (f32[16,48]{1,0:T(8,128)S(1)}, f32[16,48]{1,0:T(8,128)}, u32[]{:S(2)}) copy-start(f32[16,48]{1,0:T(8,128)} %get-tuple-element.17) | copy-start | bytes 9220
  458.7 38.1 %copy-start.2 = (f32[16,64,768]{2,1,0:T(8,128)}, f32[16,64,768]{2,1,0:T(8,128)S(1)}, u32[]{:S(2)}) copy-start(f32[16,64,768]{2,1,0:T(8,128)S(1)} %fusion.12) | copy-start | bytes 9437188
  458.8 7.8 %collective-permute-start.12 = (f32[1,64,768]{2,1,0:T(8,128)S(1)}, f32[1,64,768]{2,1,0:T(8,128)S(1)}, u32[]{:S(2)}, u32[]{:S(2)}) collective-permute-start(f32[1,64,768]{2,1,0:T(8,128)S(1)} %get-tuple-element.50), channel_id=1, source_target_pairs={{0,16},{16,32},{32,48},{48,64},{64,80},{80,96},{96,112},{112,0},{1... | collective-permute-start | bytes 589832 | tf_op jit(solution)/shard_map/ppermute | solution.py:21
  458.8 7.8 %collective-permute-start.13 = (f32[1,64,768]{2,1,0:T(8,128)S(1)}, f32[1,64,768]{2,1,0:T(8,128)S(1)}, u32[]{:S(2)}, u32[]{:S(2)}) collective-permute-start(f32[1,64,768]{2,1,0:T(8,128)S(1)} %get-tuple-element.51), channel_id=1, source_target_pairs={{16,0},{32,16},{48,32},{64,48},{80,64},{96,80},{112,96},{0,112},{1... | collective-permute-start | bytes 589832 | tf_op jit(solution)/shard_map/ppermute | solution.py:23
  467.3 26.3 %collective-permute-start.14 = (f32[18,1,768]{2,1,0:T(1,128)}, f32[18,1,768]{2,1,0:T(1,128)}, u32[]{:S(2)}, u32[]{:S(2)}) collective-permute-start(f32[18,1,768]{2,1,0:T(1,128)} %get-tuple-element.44), channel_id=1, source_target_pairs={{0,1},{1,2},{2,3},{3,4},{4,5},{5,6},{6,7},{7,8},{8,9},{9,10},{10,1... | collective-permute-start | bytes 165896 | tf_op jit(solution)/shard_map/ppermute | solution.py:21
  467.3 26.3 %collective-permute-start.15 = (f32[18,1,768]{2,1,0:T(1,128)}, f32[18,1,768]{2,1,0:T(1,128)}, u32[]{:S(2)}, u32[]{:S(2)}) collective-permute-start(f32[18,1,768]{2,1,0:T(1,128)} %get-tuple-element.45), channel_id=1, source_target_pairs={{1,0},{2,1},{3,2},{4,3},{5,4},{6,5},{7,6},{8,7},{9,8},{10,9},{11,1... | collective-permute-start | bytes 165896 | tf_op jit(solution)/shard_map/ppermute | solution.py:23
  507.4 4.7 copy-start.7
  507.4 4.7 copy-start.8
where the time goes:
time: 529 us; the launch traced here: 521 us
  other arithmetic  239 us (45%)
  local copies, waits for them, and re-layouts  152 us (29%)
  blocking collectives  47.1 us (9%)
  starting transfers between devices  38.8 us (7%)
  waiting for transfers between devices  35.7 us (7%)
  matrix products  6.39 us (1%)
    scatter-add x1, other arithmetic, on_device(): flat_flow = flat_flow.at[0, cell_ids].add(forcing * thrust)  59.7 us
    scatter-add x1, other arithmetic, on_device(): flat_flow = flat_flow.at[1, cell_ids].add(forcing * swirl_force)  59.7 us
    scatter x2, local copies, waits for them, and re-layouts, on_device(): outbox = outbox.at[target, :, rank_in].set(payload, mode='drop')  54.3 us
    ppermute x8, starting transfers between devices, extended_2(): lax.ppermute(head, axis, [((i + 1) % count, i) for i in range(count)])  36.7 us
    ppermute x8, waiting for transfers between devices, extended_2(): lax.ppermute(tail, axis, [(i, (i + 1) % count) for i in range(count)])  35.5 us
    unnamed x49, local copies, waits for them, and re-layouts  32.7 us
    sub x1, other arithmetic, on_device(): centre + viscous * (beside_all - 6.0 * centre)  29.7 us
    mul x4, other arithmetic, ghost_mask(): return extended * kept.reshape(mask_shape)  24.2 us
  transfers between devices with their start and end apart: 16, of which 8 were waited for; matrix products, arithmetic and copies ran while one was open for 3% of the time, Pallas kernels for 0%

commit v1 on v0

v1 whole, which is shorter than its diff:
```python
import functools

import jax
import jax.numpy as jnp
from jax import lax
from jax.experimental import pallas as pl
from jax.experimental.pallas import tpu as pltpu
from jax.sharding import PartitionSpec as P

MESH = pl.DeviceIdType.MESH
F32 = jnp.float32
I32 = jnp.int32
BF16 = jnp.bfloat16
L = 128
PAD = 8


def z_pair(tiles, lane):
    up = [pltpu.roll(t, L - 1, 1) for t in tiles]
    down = [pltpu.roll(t, 1, 1) for t in tiles]
    last = len(tiles) - 1
    zero = jnp.zeros_like(tiles[0])
    after = [jnp.where(lane == L - 1, up[j + 1] if j < last else zero, up[j]) for j in range(last + 1)]
    before = [jnp.where(lane == 0, down[j - 1] if j > 0 else zero, down[j]) for j in range(last + 1)]
    return after, before


def kernel(
    n_slab,
    n_sector,
    vel,
    pre,
    cell_h,
    owner_h,
    section_h,
    polar,
    geometry_h,
    count_s,
    out,
    out_s,
    loads,
    field,
    push0,
    push1,
    push_face,
    cell_s,
    owner_s,
    section_s,
    cell_v,
    owner_v,
    section_v,
    geometry,
    small_sem,
    table,
    lift_rows,
    drag_rows,
    geo0,
    geo1,
    row0,
    row1,
    rhs,
    ys1,
    yr1,
    ysp,
    yrp,
    ysm,
    yrm,
    yss,
    yrs,
    load_send,
    load_recv,
    slab_send,
    slab_recv,
    local_sem,
    polar_sem,
    x_send,
    x_recv,
    y_send,
    y_recv,
    t_send,
    t_recv,
    w_send,
    w_recv,
    l_send,
    l_recv,
    m_send,
    m_recv,
):
    sl = lax.axis_index("slab")
    se = lax.axis_index("sector")
    nx, ny, nz = pre.shape
    nj = nz // L
    slots = cell_h.shape[1]
    sec_dev = polar.shape[1]
    bins = polar.shape[2]
    has_left = sl > 0
    has_right = sl < n_slab - 1
    rows = pl.ds(PAD, ny)

    step_x = 4
    parts = nx // step_x
    order = [0, parts - 1] + list(range(1, parts - 1))

    def load(part, j):
        xs = pl.ds(part * step_x, step_x)
        xd = pl.ds(1 + part * step_x, step_x)
        zs = pl.ds(j * L, L)
        return (
            pltpu.make_async_copy(vel.at[:, xs, :, zs], field.at[0:3, xd, j, rows, :], local_sem.at[0, part, j]),
            pltpu.make_async_copy(pre.at[xs, :, zs], field.at[3, xd, j, rows, :], local_sem.at[1, part, j]),
        )

    for part in order:
        for j in range(nj):
            for c in load(part, j):
                c.start()
    polar_copies = [
        pltpu.make_async_copy(
            polar.at[:, :, pl.ds(b * L, L)], table.at[se, :, b, pl.ds(0, sec_dev), :], polar_sem.at[b]
        )
        for b in range(bins // L)
    ]
    small_copies = [
        pltpu.make_async_copy(src, dst, small_sem.at[k])
        for k, (src, dst) in enumerate(
            (
                (geometry_h, geometry),
                (cell_h, cell_s),
                (owner_h, owner_s),
                (section_h, section_s),
                (cell_h, cell_v),
                (owner_h, owner_v),
                (section_h, section_v),
            )
        )
    ]
    for c in polar_copies + small_copies:
        c.start()

    barrier = pltpu.get_barrier_semaphore()

    @pl.loop(1, n_sector)
    def _(d):
        pl.semaphore_signal(barrier, inc=1, device_id=(sl, lax.rem(se + d, n_sector)), device_id_type=MESH)

    @pl.loop(1, n_slab)
    def _(d):
        pl.semaphore_signal(barrier, inc=1, device_id=(lax.rem(sl + d, n_slab), se), device_id_type=MESH)

    def zero_plane(x):
        @pl.loop(0, nj)
        def _(j):
            for f in range(4):
                field[f, x, j, rows, :] = jnp.zeros((ny, L), F32)
            push0[x, j] = jnp.zeros((ny, L), F32)

    @pl.when(jnp.logical_not(has_left))
    def _():
        zero_plane(0)

    @pl.when(jnp.logical_not(has_right))
    def _():
        zero_plane(nx + 1)

    for c in small_copies:
        c.wait()
    load_send[...] = jnp.zeros(load_send.shape, F32)
    for c in range(2):
        for b in range(bins // L):
            table[se, c, b, sec_dev : sec_dev + 8, :] = jnp.zeros((8, L), F32)
        table[se, c, 0, sec_dev : sec_dev + 1, 0:sec_dev] = geometry[c : c + 1, :]
    for buffer in (ys1, ysp, ysm, yss):
        buffer[...] = jnp.zeros(buffer.shape, F32)
    for c in polar_copies:
        c.wait()
    pl.semaphore_wait(barrier, n_sector - 1 + n_slab - 1)

    def x_copy(stage, direction):
        kept, ghost = (1, nx + 1) if direction == 0 else (nx, 0)
        if stage == 0:
            src, dst = field.at[:, kept, :, rows, :], field.at[:, ghost, :, rows, :]
        elif stage == 1:
            src, dst = push0.at[kept], push_face.at[direction]
        else:
            src, dst = field.at[stage - 2, kept, :, rows, :], field.at[stage - 2, ghost, :, rows, :]
        return pltpu.make_async_remote_copy(
            src_ref=src,
            dst_ref=dst,
            send_sem=x_send.at[stage, direction],
            recv_sem=x_recv.at[stage, direction],
            device_id=(sl - 1 if direction == 0 else sl + 1, se),
            device_id_type=MESH,
        )

    def x_start(stage):
        @pl.when(has_left)
        def _():
            x_copy(stage, 0).start()

        @pl.when(has_right)
        def _():
            x_copy(stage, 1).start()

    def x_wait_recv(stage):
        @pl.when(has_right)
        def _():
            x_copy(stage, 0).wait_recv()

        @pl.when(has_left)
        def _():
            x_copy(stage, 1).wait_recv()

    def x_wait_send(stage):
        @pl.when(has_left)
        def _():
            x_copy(stage, 0).wait_send()

        @pl.when(has_right)
        def _():
            x_copy(stage, 1).wait_send()

    below = (sl, lax.rem(se + n_sector - 1, n_sector))
    above = (sl, lax.rem(se + 1, n_sector))

    def y_copies(slot, src, dst, at):
        return [
            pltpu.make_async_remote_copy(
                src_ref=src.at[(direction,) + at],
                dst_ref=dst.at[(direction,) + at],
                send_sem=y_send.at[slot, direction],
                recv_sem=y_recv.at[slot, direction],
                device_id=(below, above)[direction],
                device_id_type=MESH,
            )
            for direction in range(2)
        ]

    inner = (pl.ds(1, nx - 2),)
    y_all = {
        "first": y_copies(0, ys1, yr1, ()),
        "push": y_copies(1, ysp, yrp, ()),
        "mid_in": y_copies(2, ysm, yrm, inner),
        "mid_lo": y_copies(3, ysm, yrm, (0,)),
        "mid_hi": y_copies(4, ysm, yrm, (nx - 1,)),
        "set_in": y_copies(5, yss, yrs, inner),
        "set_lo": y_copies(6, yss, yrs, (0,)),
        "set_hi": y_copies(7, yss, yrs, (nx - 1,)),
    }

    def y_start(*names):
        for name in names:
            for c in y_all[name]:
                c.start()

    def y_wait_recv(*names):
        for name in names:
            for c in y_all[name]:
                c.wait_recv()

    def pack(buffer, lead, ref, lead_ref, x):
        for j in range(nj):
            buffer[(0,) + lead + (x - 1, pl.ds(j, 1))] = ref[lead_ref + (j, pl.ds(PAD, 1))]
            buffer[(1,) + lead + (x - 1, pl.ds(j, 1))] = ref[lead_ref + (j, pl.ds(PAD + ny - 1, 1))]

    def unpack(buffer, lead, ref, lead_ref, x):
        for j in range(nj):
            ref[lead_ref + (j, pl.ds(PAD + ny, 1))] = buffer[(0,) + lead + (x - 1, pl.ds(j, 1))]
            ref[lead_ref + (j, pl.ds(PAD - 1, 1))] = buffer[(1,) + lead + (x - 1, pl.ds(j, 1))]

    def table_copy(k):
        return pltpu.make_async_remote_copy(
            src_ref=table.at[se],
            dst_ref=table.at[se],
            send_sem=t_send.at[k],
            recv_sem=t_recv.at[k],
            device_id=(sl, lax.rem(se + 2 * k, n_sector)),
            device_id_type=MESH,
        )

    twin = se + 1 - 2 * lax.rem(se, 2)

    def twin_copy(k):
        block = lax.rem(se + n_sector - 2 * k, n_sector)
        return pltpu.make_async_remote_copy(
            src_ref=table.at[block],
            dst_ref=table.at[block],
            send_sem=w_send.at[k],
            recv_sem=w_recv.at[k],
            device_id=(sl, twin),
            device_id_type=MESH,
        )

    half = n_sector // 2

    for count, part in enumerate(order):
        for j in range(nj):
            for c in load(part, j):
                c.wait()
        if count == 1:
            x_start(0)

    @pl.loop(1, nx + 1)
    def _(x):
        for f in range(4):
            pack(ys1, (f,), field, (f, x), x)

    y_start("first")

    @pl.loop(1, half)
    def _(k):
        table_copy(k).start()

    twin_copy(0).start()

    lane = lax.broadcasted_iota(I32, (8, L), 1)

    def plane_of(i):
        return jnp.where(i < nx - 2, i + 2, jnp.where(i == nx - 2, 1, nx))

    y_wait_recv("first")

    @pl.loop(0, nx)
    def _(i):
        x = plane_of(i)

        @pl.when(i == nx - 2)
        def _():
            x_wait_recv(0)

        for f in range(4):
            unpack(yr1, (f,), field, (f, x), x)
        for y in range(0, ny, 8):
            here = pl.ds(PAD + y, 8)

            def sides(f, j):
                return (
                    field[f, x + 1, j, here, :],
                    field[f, x - 1, j, here, :],
                    field[f, x, j, pl.ds(PAD + y + 1, 8), :],
                    field[f, x, j, pl.ds(PAD + y - 1, 8), :],
                )

            centre = [field[3, x, j, here, :] for j in range(nj)]
            after, before = z_pair(centre, lane)
            slope = []
            for j in range(nj):
                xp, xm, yp, ym = sides(3, j)
                out_s[x - 1, pl.ds(y, 8), pl.ds(j * L, L)] = (xp + xm) + (yp + ym) + (after[j] + before[j])
                slope.append((xp - xm, yp - ym, after[j] - before[j]))
            for f in range(3):
                centre = [field[f, x, j, here, :] for j in range(nj)]
                after, before = z_pair(centre, lane)
                for j in range(nj):
                    xp, xm, yp, ym = sides(f, j)
                    total = (xp + xm) + (yp + ym) + (after[j] + before[j])
                    value = 0.4 * centre[j] + 0.1 * total - 0.25 * slope[j][f]
                    if f == 0:
                        push0[x, j, pl.ds(y, 8), :] = value
                    elif f == 1:
                        push1[x - 1, j, here, :] = value
                    else:
                        out[2, x - 1, pl.ds(y, 8), pl.ds(j * L, L)] = value

    @pl.loop(1, half)
    def _(k):
        table_copy(k).wait_recv()
        twin_copy(k).start()

    @pl.loop(0, half)
    def _(k):
        twin_copy(k).wait_recv()

    @pl.loop(0, slots, unroll=4)
    def _(s):
        cell = cell_s[0, s]
        xy = ((cell >> 8) * 21846) >> 16
        z = cell - nz * xy
        x = xy >> 6
        y = xy & (ny - 1)
        j = z >> 7
        owner = owner_s[0, s]
        section = section_s[0, s]
        at = pl.ds(s, 1)
        row0[at, :] = push0[x + 1, j, pl.ds(y, 1), :]
        row1[at, :] = push1[x, j, pl.ds(y + PAD, 1), :]
        for b in range(bins // L):
            lift_rows[b, at, :] = table[owner, 0, b, pl.ds(section, 1), :]
            drag_rows[b, at, :] = table[owner, 1, b, pl.ds(section, 1), :]
        geo0[at, :] = table[owner, 0, 0, pl.ds(sec_dev, 1), :]
        geo1[at, :] = table[owner, 1, 0, pl.ds(sec_dev, 1), :]

    diagonal = lax.broadcasted_iota(I32, (L, L), 0) == lax.broadcasted_iota(I32, (L, L), 1)
    lanes = lax.broadcasted_iota(I32, (L, L), 1).astype(F32)
    z_ids = lax.broadcasted_iota(I32, (L, nz), 1).astype(F32)
    places = lax.broadcasted_iota(I32, (L, 1), 0)
    used = count_s[0, 0]

    def column(row):
        return jnp.sum(jnp.where(diagonal, row, 0.0), axis=1, keepdims=True)

    def picked(block, lane_of):
        return jnp.sum(jnp.where(lanes == lane_of, block, 0.0), axis=1, keepdims=True)

    def xy_of(cell):
        return (((cell >> 8).astype(F32) + 0.5) * (1.0 / 3.0)).astype(I32)

    for g in range(slots // L):
        at = pl.ds(g * L, L)
        cell = cell_v[0:1, at]
        z_row = cell - nz * xy_of(cell)
        z_col = column(z_row.astype(F32))
        lane_col = column((z_row & (L - 1)).astype(F32))
        section = column(section_v[0:1, at].astype(F32))
        whole = column((owner_v[0:1, at] * sec_dev + section_v[0:1, at]).astype(F32))
        radius = 0.25 + 0.75 * (z_col + 0.5) / nz
        a = 1.0 + picked(row0[at, :], lane_col)
        t = 10.0 * radius + picked(row1[at, :], lane_col)
        chord = picked(geo0[at, :], section)
        twist = picked(geo1[at, :], section)
        position = (jnp.arctan2(a, t) - twist + 2.0) * ((bins - 1) / 4.0)
        lift, drag = 0.0, 0.0
        for b in range(bins // L):
            weight = jnp.maximum(0.0, 1.0 - jnp.abs(position - (lanes + float(b * L))))
            lift = lift + lift_rows[b, at, :] * weight
            drag = drag + drag_rows[b, at, :] * weight
        lift = jnp.sum(lift, axis=1, keepdims=True)
        drag = jnp.sum(drag, axis=1, keepdims=True)
        scale = 0.5 * chord * jnp.sqrt(a * a + t * t)
        active = places + g * L < used
        thrust = jnp.where(active, scale * (lift * t - drag * a), 0.0)
        swirl = jnp.where(active, scale * (lift * a + drag * t), 0.0)
        torque = swirl * radius
        mask = z_ids == z_col
        for c, force in ((0, 0.2 * thrust), (1, 0.2 * swirl)):
            high = force.astype(BF16).astype(F32)
            rhs[c, 0, at, :] = jnp.where(mask, high, 0.0).astype(BF16)
            rhs[c, 1, at, :] = jnp.where(mask, force - high, 0.0).astype(BF16)
        for pair in range(half):
            chosen = lanes == whole - float(pair * L)
            load_send[pair, 0:1, :] += jnp.sum(jnp.where(chosen, thrust, 0.0), axis=0, keepdims=True)
            load_send[pair, 1:2, :] += jnp.sum(jnp.where(chosen, torque, 0.0), axis=0, keepdims=True)

    def load_copy(d):
        peer = lax.rem(se + d, n_sector)
        return pltpu.make_async_remote_copy(
            src_ref=load_send.at[peer // 2],
            dst_ref=load_recv.at[se],
            send_sem=l_send.at[d],
            recv_sem=l_recv.at[d],
            device_id=(sl, peer),
            device_id_type=MESH,
        )

    def slab_copy(d):
        return pltpu.make_async_remote_copy(
            src_ref=slab_send,
            dst_ref=slab_recv.at[sl],
            send_sem=m_send.at[d],
            recv_sem=m_recv.at[d],
            device_id=(lax.rem(sl + d, n_slab), se),
            device_id_type=MESH,
        )

    chunk = 4
    high_rows = lax.broadcasted_iota(I32, (chunk * ny, slots), 0)
    xy_all = xy_of(cell_v[...])

    @pl.loop(0, nx // chunk)
    def _(i):
        m = jnp.where(i == 0, 0, jnp.where(i == 1, nx // chunk - 1, i - 1))
        chosen = jnp.where(high_rows == xy_all - m * (chunk * ny), 1.0, 0.0).astype(BF16)
        for c in range(2):
            total = jnp.dot(chosen, rhs[c, 0], preferred_element_type=F32) + jnp.dot(
                chosen, rhs[c, 1], preferred_element_type=F32
            )
            for k in range(chunk):
                for j in range(nj):
                    piece = total[k * ny : (k + 1) * ny, j * L : (j + 1) * L]
                    if c == 0:
                        push0[1 + m * chunk + k, j] += piece
                    else:
                        push1[m * chunk + k, j, rows, :] += piece

        @pl.when(i == 1)
        def _():
            x_start(1)

    @pl.loop(1, nx + 1)
    def _(x):
        pack(ysp, (), push1, (x - 1,), x)

    y_start("push")

    @pl.loop(1, n_sector)
    def _(d):
        load_copy(d).start()

    load_recv[se] = load_send[se // 2]

    y_wait_recv("push")
    x_wait_send(0)

    @pl.loop(0, nx)
    def _(i):
        x = plane_of(i)

        @pl.when(i == nx - 2)
        def _():
            y_start("mid_in")
            x_wait_recv(1)
            for direction, there, ghost in ((0, has_right, nx + 1), (1, has_left, 0)):

                @pl.when(there)
                def _():
                    for j in range(nj):
                        push0[ghost, j] = push_face[direction, j]


        unpack(yrp, (), push1, (x - 1,), x)
        for y in range(0, ny, 8):
            ys = pl.ds(y, 8)
            after, before = z_pair([out[2, x - 1, ys, pl.ds(j * L, L)] for j in range(nj)], lane)
            for j in range(nj):
                source = 0.5 * (
                    (push0[x + 1, j, ys, :] - push0[x - 1, j, ys, :])
                    + (push1[x - 1, j, pl.ds(PAD + y + 1, 8), :] - push1[x - 1, j, pl.ds(PAD + y - 1, 8), :])
                    + (after[j] - before[j])
                )
                middle = (out_s[x - 1, ys, pl.ds(j * L, L)] - source) * (1.0 / 6.0)
                field[0, x, j, pl.ds(PAD + y, 8), :] = middle
                out_s[x - 1, ys, pl.ds(j * L, L)] = source
        pack(ysm, (), field, (0, x), x)

    x_start(2)
    y_start("mid_lo", "mid_hi")

    @pl.loop(1, n_sector)
    def _(d):
        load_copy(d).wait_recv()

    mine = load_recv[0]
    for d in range(1, n_sector):
        mine = mine + load_recv[d]
    mine = jnp.where(lax.rem(se, 2) == 1, pltpu.roll(mine, L // 2, 1), mine)
    slab_send[...] = mine
    slab_recv[sl] = mine

    @pl.loop(1, n_slab)
    def _(d):
        slab_copy(d).start()

    y_wait_recv("mid_in")

    @pl.loop(0, nx)
    def _(i):
        x = plane_of(i)

        @pl.when(i == nx - 2)
        def _():
            y_start("set_in")
            y_wait_recv("mid_lo", "mid_hi")
            x_wait_recv(2)

        unpack(yrm, (), field, (0, x), x)
        for y in range(0, ny, 8):
            ys = pl.ds(y, 8)
            here = pl.ds(PAD + y, 8)
            after, before = z_pair([field[0, x, j, here, :] for j in range(nj)], lane)
            for j in range(nj):
                total = (
                    (field[0, x + 1, j, here, :] + field[0, x - 1, j, here, :])
                    + (field[0, x, j, pl.ds(PAD + y + 1, 8), :] + field[0, x, j, pl.ds(PAD + y - 1, 8), :])
                    + (after[j] + before[j])
                )
                settled = (total - out_s[x - 1, ys, pl.ds(j * L, L)]) * (1.0 / 6.0)
                field[1, x, j, here, :] = settled
                out_s[x - 1, ys, pl.ds(j * L, L)] = settled
        pack(yss, (), field, (1, x), x)

    x_start(3)
    y_start("set_lo", "set_hi")

    y_wait_recv("set_in")

    @pl.loop(0, nx)
    def _(i):
        x = plane_of(i)

        @pl.when(i == nx - 2)
        def _():
            y_wait_recv("set_lo", "set_hi")
            x_wait_recv(3)

        unpack(yrs, (), field, (1, x), x)
        for y in range(0, ny, 8):
            ys = pl.ds(y, 8)
            here = pl.ds(PAD + y, 8)
            after, before = z_pair([field[1, x, j, here, :] for j in range(nj)], lane)
            for j in range(nj):
                zs = pl.ds(j * L, L)
                out[0, x - 1, ys, zs] = push0[x, j, ys, :] - 0.5 * (field[1, x + 1, j, here, :] - field[1, x - 1, j, here, :])
                out[1, x - 1, ys, zs] = push1[x - 1, j, here, :] - 0.5 * (
                    field[1, x, j, pl.ds(PAD + y + 1, 8), :] - field[1, x, j, pl.ds(PAD + y - 1, 8), :]
                )
                out[2, x - 1, ys, zs] = out[2, x - 1, ys, zs] - 0.5 * (after[j] - before[j])

    @pl.loop(1, n_slab)
    def _(d):
        slab_copy(d).wait_recv()

    final = slab_recv[0]
    for d in range(1, n_slab):
        final = final + slab_recv[d]
    loads[...] = final[0:2, 0:sec_dev]

    for stage in range(1, 4):
        x_wait_send(stage)
    for copies in y_all.values():
        for c in copies:
            c.wait_send()

    @pl.loop(1, half)
    def _(k):
        table_copy(k).wait_send()

    @pl.loop(0, half)
    def _(k):
        twin_copy(k).wait_send()

    @pl.loop(1, n_sector)
    def _(d):
        load_copy(d).wait_send()

    @pl.loop(1, n_slab)
    def _(d):
        slab_copy(d).wait_send()


def on_device(n_slab, n_sector, velocity, pressure, disk_cell, disk_count, disk_owner, disk_section, polar, geometry):
    nx, ny, nz = pressure.shape
    nj = nz // L
    slots = disk_cell.shape[1]
    sec_dev, bins = polar.shape[1:]
    tall = ny + 2 * PAD
    owner = disk_owner.reshape(1, slots)
    dma = pltpu.SemaphoreType.DMA
    hbm = pl.BlockSpec(memory_space=pltpu.HBM)
    vmem = pl.BlockSpec(memory_space=pltpu.VMEM)
    half = n_sector // 2
    corrected, settled, loads = pl.pallas_call(
        functools.partial(kernel, n_slab, n_sector),
        out_shape=(
            pltpu.VMEM((3, nx, ny, nz), F32),
            pltpu.VMEM((nx, ny, nz), F32),
            jax.ShapeDtypeStruct((2, sec_dev), F32),
        ),
        in_specs=[hbm] * 7 + [pl.BlockSpec(memory_space=pltpu.SMEM)],
        out_specs=(vmem, vmem, vmem),
        scratch_shapes=[
            pltpu.VMEM((4, nx + 2, nj, tall, L), F32),
            pltpu.VMEM((nx + 2, nj, ny, L), F32),
            pltpu.VMEM((nx, nj, tall, L), F32),
            pltpu.VMEM((2, nj, ny, L), F32),
            pltpu.SMEM((1, slots), jnp.int32),
            pltpu.SMEM((1, slots), jnp.int32),
            pltpu.SMEM((1, slots), jnp.int32),
            pltpu.VMEM((1, slots), jnp.int32),
            pltpu.VMEM((1, slots), jnp.int32),
            pltpu.VMEM((1, slots), jnp.int32),
            pltpu.VMEM((2, sec_dev), F32),
            dma((8,)),
            pltpu.VMEM((n_sector, 2, bins // L, sec_dev + 8, L), F32),
            pltpu.VMEM((bins // L, slots, L), F32),
            pltpu.VMEM((bins // L, slots, L), F32),
            pltpu.VMEM((slots, L), F32),
            pltpu.VMEM((slots, L), F32),
            pltpu.VMEM((slots, L), F32),
            pltpu.VMEM((slots, L), F32),
            pltpu.VMEM((2, 2, slots, nz), BF16),
            pltpu.VMEM((2, 4, nx, 8, L), F32),
            pltpu.VMEM((2, 4, nx, 8, L), F32),
            pltpu.VMEM((2, nx, 8, L), F32),
            pltpu.VMEM((2, nx, 8, L), F32),
            pltpu.VMEM((2, nx, 8, L), F32),
            pltpu.VMEM((2, nx, 8, L), F32),
            pltpu.VMEM((2, nx, 8, L), F32),
            pltpu.VMEM((2, nx, 8, L), F32),
            pltpu.VMEM((half, 8, L), F32),
            pltpu.VMEM((n_sector, 8, L), F32),
            pltpu.VMEM((8, L), F32),
            pltpu.VMEM((n_slab, 8, L), F32),
            dma((2, nx // 4, nj)),
            dma((bins // L,)),
            dma((4, 2)),
            dma((4, 2)),
            dma((8, 2)),
            dma((8, 2)),
            dma((half,)),
            dma((half,)),
            dma((half,)),
            dma((half,)),
            dma((n_sector,)),
            dma((n_sector,)),
            dma((n_slab,)),
            dma((n_slab,)),
        ],
        compiler_params=pltpu.CompilerParams(
            collective_id=0, has_side_effects=True, vmem_limit_bytes=40 * 1024 * 1024
        ),
    )(
        *(
            pltpu.with_memory_space_constraint(array, pltpu.HBM)
            for array in (velocity, pressure, disk_cell, owner, disk_section, polar, geometry)
        ),
        disk_count,
    )
    return corrected, settled, loads


def solution(mesh):
    return jax.shard_map(
        functools.partial(on_device, mesh.shape["slab"], mesh.shape["sector"]),
        mesh=mesh,
        in_specs=(
            P(None, "slab", "sector", None),
            P("slab", "sector", None),
            P("slab", "sector"),
            P("slab", "sector"),
            P("slab", "sector", None),
            P("slab", "sector"),
            P(None, "sector", None),
            P(None, "sector"),
        ),
        out_specs=(P(None, "slab", "sector", None), P("slab", "sector", None), P(None, "sector")),
        check_vma=False,
    )
```

time: 529 us -> 95.5 us (0.18)
  the two profiles are of different devices: /device:TPU:0 before, /device:TPU:30 now
where the time goes in v1:
time: 95.5 us; the launch traced here: 95.4 us
  Pallas kernels  88.1 us (92%)
  local copies, waits for them, and re-layouts  5.97 us (6%)
  between operations  1.29 us (1%)
    pallas_call x1, Pallas kernels, on_device(): pl.pallas_call(functools.partial(kernel, n_slab, n_sector), out_shape=(pl...  88.1 us
    unnamed x3, local copies, waits for them, and re-layouts  5.97 us

profile of v1, /device:TPU:30, one launch (start us, length us, event | category | flops | bytes accessed | tf_op | source)
XLA Modules:
  0.0 95.4 jit_solution(10650564548114220510)
XLA Ops:
  1.3 88.1 %shard_map.103 = (f32[3,16,64,768]{3,2,1,0:T(8,128)S(1)}, f32[16,64,768]{2,1,0:T(8,128)S(1)}, f32[2,64]{1,0:T(2,128)S(1)}) custom-call(f32[3,16,64,768]{3,2,1,0:T(8,128)} %vel.1, f32[16,64,768]{2,1,0:T(8,128)} %pre.1, s32[1,512]{1,0:T(1,128)} %cell_h.1, s32[1,512]{1,0:T(1,128)} %bitcast.1, s32[1,512]{1,0:T(1,128)} %section_h.1, f32[2,64,256]{2,1,0:T(8,128)} %polar.1, ...), custom_call_target="tpu_custom_call" | custom-call | tf_op jit(solution)/shard_map/pallas_call | solution.py:650
  89.4 3.7 %copy.14 = f32[3,16,64,768]{3,2,1,0:T(8,128)} copy(f32[3,16,64,768]{3,2,1,0:T(8,128)S(1)} %get-tuple-element.3) | data formatting | bytes 18874368
  93.1 1.7 %copy.15 = f32[16,64,768]{2,1,0:T(8,128)} copy(f32[16,64,768]{2,1,0:T(8,128)S(1)} %get-tuple-element.4) | data formatting | bytes 6291456
  94.8 0.6 copy.17

commit v2 on v1

--- a/solution.py
+++ b/solution.py
@@ -42,7 +42,8 @@
     field,
     push0,
     push1,
-    push_face,
+    x_out,
+    x_in,
     cell_s,
     owner_s,
     section_s,
@@ -59,14 +60,10 @@
     row0,
     row1,
     rhs,
-    ys1,
-    yr1,
-    ysp,
-    yrp,
-    ysm,
-    yrm,
-    yss,
-    yrs,
+    first_out,
+    first_in,
+    y_out,
+    y_in,
     load_send,
     load_recv,
     slab_send,
@@ -97,20 +94,19 @@
     has_right = sl < n_slab - 1
     rows = pl.ds(PAD, ny)
 
-    step_x = 4
-    parts = nx // step_x
-    order = [0, parts - 1] + list(range(1, parts - 1))
+    parts = ((0, 1), (nx - 1, 1), (1, nx // 2 - 1), (nx // 2, nx // 2 - 1))
 
     def load(part, j):
-        xs = pl.ds(part * step_x, step_x)
-        xd = pl.ds(1 + part * step_x, step_x)
+        start, count = parts[part]
+        xs = pl.ds(start, count)
+        xd = pl.ds(1 + start, count)
         zs = pl.ds(j * L, L)
         return (
             pltpu.make_async_copy(vel.at[:, xs, :, zs], field.at[0:3, xd, j, rows, :], local_sem.at[0, part, j]),
             pltpu.make_async_copy(pre.at[xs, :, zs], field.at[3, xd, j, rows, :], local_sem.at[1, part, j]),
         )
 
-    for part in order:
+    for part in range(len(parts)):
         for j in range(nj):
             for c in load(part, j):
                 c.start()
@@ -147,20 +143,21 @@
     def _(d):
         pl.semaphore_signal(barrier, inc=1, device_id=(lax.rem(sl + d, n_slab), se), device_id_type=MESH)
 
-    def zero_plane(x):
+    @pl.loop(1, nx + 1)
+    def _(x):
+        for beyond in (0, PAD + ny):
+            for j in range(nj):
+                for f in range(4):
+                    field[f, x, j, beyond : beyond + PAD, :] = jnp.zeros((PAD, L), F32)
+                push1[x - 1, j, beyond : beyond + PAD, :] = jnp.zeros((PAD, L), F32)
+
+    for ghost in (0, nx + 1):
+
         @pl.loop(0, nj)
         def _(j):
             for f in range(4):
-                field[f, x, j, rows, :] = jnp.zeros((ny, L), F32)
-            push0[x, j] = jnp.zeros((ny, L), F32)
-
-    @pl.when(jnp.logical_not(has_left))
-    def _():
-        zero_plane(0)
-
-    @pl.when(jnp.logical_not(has_right))
-    def _():
-        zero_plane(nx + 1)
+                field[f, ghost, j, rows, :] = jnp.zeros((ny, L), F32)
+            push0[ghost, j] = jnp.zeros((ny, L), F32)
 
     for c in small_copies:
         c.wait()
@@ -169,29 +166,36 @@
         for b in range(bins // L):
             table[se, c, b, sec_dev : sec_dev + 8, :] = jnp.zeros((8, L), F32)
         table[se, c, 0, sec_dev : sec_dev + 1, 0:sec_dev] = geometry[c : c + 1, :]
-    for buffer in (ys1, ysp, ysm, yss):
+    for buffer in (first_out, y_out):
         buffer[...] = jnp.zeros(buffer.shape, F32)
-    for c in polar_copies:
-        c.wait()
-    pl.semaphore_wait(barrier, n_sector - 1 + n_slab - 1)
+    W0, V1, V2, MID, SET, COR = range(6)
 
     def x_copy(stage, direction):
-        kept, ghost = (1, nx + 1) if direction == 0 else (nx, 0)
-        if stage == 0:
-            src, dst = field.at[:, kept, :, rows, :], field.at[:, ghost, :, rows, :]
-        elif stage == 1:
-            src, dst = push0.at[kept], push_face.at[direction]
+        kept = 1 if direction == 0 else nx
+        if stage in (V1, V2):
+            src = field.at[stage, kept, :, rows, :]
+        elif stage == COR:
+            src = field.at[1, kept, :, rows, :]
         else:
-            src, dst = field.at[stage - 2, kept, :, rows, :], field.at[stage - 2, ghost, :, rows, :]
+            src = x_out.at[{W0: 0, MID: 1, SET: 2}[stage], direction]
         return pltpu.make_async_remote_copy(
             src_ref=src,
-            dst_ref=dst,
+            dst_ref=x_in.at[stage, direction],
             send_sem=x_send.at[stage, direction],
             recv_sem=x_recv.at[stage, direction],
             device_id=(sl - 1 if direction == 0 else sl + 1, se),
             device_id_type=MESH,
         )
 
+    def x_faces(body):
+        for direction, there, kept in ((0, has_right, nx), (1, has_left, 1)):
+
+            @pl.when(there)
+            def _():
+                @pl.loop(0, nj)
+                def _(j):
+                    body(direction, kept, j)
+
     def x_start(stage):
         @pl.when(has_left)
         def _():
@@ -222,113 +226,139 @@
     below = (sl, lax.rem(se + n_sector - 1, n_sector))
     above = (sl, lax.rem(se + 1, n_sector))
 
-    def y_copies(slot, src, dst, at):
+    def y_copies(stage):
         return [
             pltpu.make_async_remote_copy(
-                src_ref=src.at[(direction,) + at],
-                dst_ref=dst.at[(direction,) + at],
-                send_sem=y_send.at[slot, direction],
-                recv_sem=y_recv.at[slot, direction],
+                src_ref=first_out.at[direction] if stage == 0 else y_out.at[stage - 1, direction],
+                dst_ref=first_in.at[direction] if stage == 0 else y_in.at[stage - 1, direction],
+                send_sem=y_send.at[stage, direction],
+                recv_sem=y_recv.at[stage, direction],
                 device_id=(below, above)[direction],
                 device_id_type=MESH,
             )
             for direction in range(2)
         ]
 
-    inner = (pl.ds(1, nx - 2),)
-    y_all = {
-        "first": y_copies(0, ys1, yr1, ()),
-        "push": y_copies(1, ysp, yrp, ()),
-        "mid_in": y_copies(2, ysm, yrm, inner),
-        "mid_lo": y_copies(3, ysm, yrm, (0,)),
-        "mid_hi": y_copies(4, ysm, yrm, (nx - 1,)),
-        "set_in": y_copies(5, yss, yrs, inner),
-        "set_lo": y_copies(6, yss, yrs, (0,)),
-        "set_hi": y_copies(7, yss, yrs, (nx - 1,)),
-    }
-
-    def y_start(*names):
-        for name in names:
-            for c in y_all[name]:
-                c.start()
-
-    def y_wait_recv(*names):
-        for name in names:
-            for c in y_all[name]:
-                c.wait_recv()
-
-    def pack(buffer, lead, ref, lead_ref, x):
-        for j in range(nj):
-            buffer[(0,) + lead + (x - 1, pl.ds(j, 1))] = ref[lead_ref + (j, pl.ds(PAD, 1))]
-            buffer[(1,) + lead + (x - 1, pl.ds(j, 1))] = ref[lead_ref + (j, pl.ds(PAD + ny - 1, 1))]
-
-    def unpack(buffer, lead, ref, lead_ref, x):
-        for j in range(nj):
-            ref[lead_ref + (j, pl.ds(PAD + ny, 1))] = buffer[(0,) + lead + (x - 1, pl.ds(j, 1))]
-            ref[lead_ref + (j, pl.ds(PAD - 1, 1))] = buffer[(1,) + lead + (x - 1, pl.ds(j, 1))]
+    y_all = [y_copies(stage) for stage in range(4)]
+
+    def y_start(stage):
+        for c in y_all[stage]:
+            c.start()
+
+    def y_wait_recv(stage):
+        for c in y_all[stage]:
+            c.wait_recv()
+
+    edges = ((0, 0, -1.0), (1, ny - 1, 1.0))
+    far_edges = ((0, ny - 1, -1.0), (1, 0, 1.0))
+
+    def y_rows(places, body):
+        @pl.loop(1, nx + 1)
+        def _(x):
+            for j in range(nj):
+                for direction, y, sign in places:
+                    body(direction, y, sign, x, j)
+
+    core = lax.rem(se, 2)
+    tall_z = n_sector // 4
+    z_here = lax.rem(se // 2, tall_z)
+    y_here = se // (2 * tall_z)
+
+    def at_step(dy, dz):
+        return lax.rem(y_here + dy, 2) * (2 * tall_z) + lax.rem(z_here + dz, tall_z) * 2 + core
+
+    down, up = tall_z - 1, 1
+    relay_from = down + (up - down) * core
+    relay_to = up + (down - up) * core
 
     def table_copy(k):
+        block, target = (
+            ((0, 0), (1, 0)),
+            ((0, 0), (0, up)),
+            ((0, 0), (0, down)),
+            ((1, 0), (0, up)),
+            ((1, 0), (0, down)),
+            ((0, relay_from), (0, relay_to)),
+            ((1, relay_from), (0, relay_to)),
+        )[k]
         return pltpu.make_async_remote_copy(
-            src_ref=table.at[se],
-            dst_ref=table.at[se],
+            src_ref=table.at[at_step(*block)],
+            dst_ref=table.at[at_step(*block)],
             send_sem=t_send.at[k],
             recv_sem=t_recv.at[k],
-            device_id=(sl, lax.rem(se + 2 * k, n_sector)),
+            device_id=(sl, at_step(*target)),
             device_id_type=MESH,
         )
 
-    twin = se + 1 - 2 * lax.rem(se, 2)
-
-    def twin_copy(k):
-        block = lax.rem(se + n_sector - 2 * k, n_sector)
+    twin = se + 1 - 2 * core
+
+    def twin_copy(dy, dz):
         return pltpu.make_async_remote_copy(
-            src_ref=table.at[block],
-            dst_ref=table.at[block],
-            send_sem=w_send.at[k],
-            recv_sem=w_recv.at[k],
+            src_ref=table.at[at_step(dy, dz)],
+            dst_ref=table.at[at_step(dy, dz)],
+            send_sem=w_send.at[dy * tall_z + dz],
+            recv_sem=w_recv.at[dy * tall_z + dz],
             device_id=(sl, twin),
             device_id_type=MESH,
         )
 
+    twins = [twin_copy(dy, dz) for dy in range(2) for dz in range(tall_z)]
+
     half = n_sector // 2
 
-    for count, part in enumerate(order):
+    def wait_part(part):
         for j in range(nj):
             for c in load(part, j):
                 c.wait()
-        if count == 1:
-            x_start(0)
+
+    wait_part(0)
+    wait_part(1)
+
+    @pl.loop(0, nj)
+    def _(j):
+        for direction, kept, sign in ((0, 1, -0.25), (1, nx, 0.25)):
+            x_out[0, direction, j] = 0.1 * field[0, kept, j, rows, :] + sign * field[3, kept, j, rows, :]
+
+    pl.semaphore_wait(barrier, n_sector - 1 + n_slab - 1)
+    x_start(W0)
+    x_start(V1)
+    for c in polar_copies:
+        c.wait()
+    for k in range(3):
+        table_copy(k).start()
+    twin_copy(0, 0).start()
+    wait_part(2)
+    wait_part(3)
+
+    def pack_first(direction, y, sign, x, j):
+        at = pl.ds(PAD + y, 1)
+        to = (x - 1, pl.ds(j, 1))
+        first_out[(direction, 0) + to] = 0.1 * field[0, x, j, at, :]
+        first_out[(direction, 1) + to] = 0.1 * field[1, x, j, at, :] + (0.25 * sign) * field[3, x, j, at, :]
+        first_out[(direction, 2) + to] = 0.1 * field[2, x, j, at, :]
+
+    y_rows(edges, pack_first)
+    y_start(0)
+
+    lane = lax.broadcasted_iota(I32, (8, L), 1)
 
     @pl.loop(1, nx + 1)
     def _(x):
-        for f in range(4):
-            pack(ys1, (f,), field, (f, x), x)
-
-    y_start("first")
-
-    @pl.loop(1, half)
-    def _(k):
-        table_copy(k).start()
-
-    twin_copy(0).start()
-
-    lane = lax.broadcasted_iota(I32, (8, L), 1)
-
-    def plane_of(i):
-        return jnp.where(i < nx - 2, i + 2, jnp.where(i == nx - 2, 1, nx))
-
-    y_wait_recv("first")
-
-    @pl.loop(0, nx)
-    def _(i):
-        x = plane_of(i)
-
-        @pl.when(i == nx - 2)
-        def _():
-            x_wait_recv(0)
-
-        for f in range(4):
-            unpack(yr1, (f,), field, (f, x), x)
+        @pl.when(x == nx // 2 + 1)
+        def _():
+            table_copy(1).wait_recv()
+            table_copy(2).wait_recv()
+            table_copy(5).start()
+            twin_copy(0, up).start()
+            twin_copy(0, down).start()
+
+        @pl.when(x == nx // 2 + 4)
+        def _():
+            table_copy(0).wait_recv()
+            table_copy(3).start()
+            table_copy(4).start()
+            twin_copy(1, 0).start()
+
         for y in range(0, ny, 8):
             here = pl.ds(PAD + y, 8)
 
@@ -361,14 +391,31 @@
                     else:
                         out[2, x - 1, pl.ds(y, 8), pl.ds(j * L, L)] = value
 
-    @pl.loop(1, half)
-    def _(k):
-        table_copy(k).wait_recv()
-        twin_copy(k).start()
-
-    @pl.loop(0, half)
-    def _(k):
-        twin_copy(k).wait_recv()
+    table_copy(5).wait_recv()
+    twin_copy(0, 2).start()
+    table_copy(3).wait_recv()
+    table_copy(4).wait_recv()
+    table_copy(6).start()
+    twin_copy(1, up).start()
+    twin_copy(1, down).start()
+    x_wait_recv(W0)
+    x_wait_recv(V1)
+    x_start(V2)
+    y_wait_recv(0)
+
+    def add_first(direction, kept, j):
+        push0[kept, j] += x_in[W0, direction, j]
+        push1[kept - 1, j, rows, :] += 0.1 * x_in[V1, direction, j]
+
+    x_faces(add_first)
+
+    def add_first_rows(direction, y, sign, x, j):
+        at = (x - 1, pl.ds(j, 1))
+        push0[x, j, pl.ds(y, 1), :] += first_in[(direction, 0) + at]
+        push1[x - 1, j, pl.ds(PAD + y, 1), :] += first_in[(direction, 1) + at]
+        out[2, x - 1, pl.ds(y, 1), pl.ds(j * L, L)] += first_in[(direction, 2) + at]
+
+    y_rows(far_edges, add_first_rows)
 
     @pl.loop(0, slots, unroll=4)
     def _(s):
@@ -378,11 +425,20 @@
         x = xy >> 6
         y = xy & (ny - 1)
         j = z >> 7
+        at = pl.ds(s, 1)
+        row0[at, :] = push0[x + 1, j, pl.ds(y, 1), :]
+        row1[at, :] = push1[x, j, pl.ds(y + PAD, 1), :]
+
+    table_copy(6).wait_recv()
+    twin_copy(1, 2).start()
+    for c in twins:
+        c.wait_recv()
+
+    @pl.loop(0, slots, unroll=4)
+    def _(s):
         owner = owner_s[0, s]
         section = section_s[0, s]
         at = pl.ds(s, 1)
-        row0[at, :] = push0[x + 1, j, pl.ds(y, 1), :]
-        row1[at, :] = push1[x, j, pl.ds(y + PAD, 1), :]
         for b in range(bins // L):
             lift_rows[b, at, :] = table[owner, 0, b, pl.ds(section, 1), :]
             drag_rows[b, at, :] = table[owner, 1, b, pl.ds(section, 1), :]
@@ -483,13 +539,19 @@
 
         @pl.when(i == 1)
         def _():
-            x_start(1)
-
-    @pl.loop(1, nx + 1)
-    def _(x):
-        pack(ysp, (), push1, (x - 1,), x)
-
-    y_start("push")
+            @pl.loop(0, nj)
+            def _(j):
+                for direction, kept, sign in ((0, 1, -0.5), (1, nx, 0.5)):
+                    x_out[1, direction, j] = field[3, kept, j, rows, :] + sign * push0[kept, j]
+
+            x_start(MID)
+
+    def pack_middle(direction, y, sign, x, j):
+        at = pl.ds(PAD + y, 1)
+        y_out[0, direction, x - 1, pl.ds(j, 1)] = field[3, x, j, at, :] + (0.5 * sign) * push1[x - 1, j, at, :]
+
+    y_rows(edges, pack_middle)
+    y_start(1)
 
     @pl.loop(1, n_sector)
     def _(d):
@@ -497,26 +559,19 @@
 
     load_recv[se] = load_send[se // 2]
 
-    y_wait_recv("push")
-    x_wait_send(0)
-
-    @pl.loop(0, nx)
-    def _(i):
-        x = plane_of(i)
-
-        @pl.when(i == nx - 2)
-        def _():
-            y_start("mid_in")
-            x_wait_recv(1)
-            for direction, there, ghost in ((0, has_right, nx + 1), (1, has_left, 0)):
-
-                @pl.when(there)
-                def _():
-                    for j in range(nj):
-                        push0[ghost, j] = push_face[direction, j]
-
-
-        unpack(yrp, (), push1, (x - 1,), x)
+    x_wait_recv(V2)
+
+    def add_depth(direction, kept, j):
+        for k in range(nj):
+
+            @pl.when(j == k)
+            def _():
+                out[2, kept - 1, :, pl.ds(k * L, L)] += 0.1 * x_in[V2, direction, k]
+
+    x_faces(add_depth)
+
+    @pl.loop(1, nx + 1)
+    def _(x):
         for y in range(0, ny, 8):
             ys = pl.ds(y, 8)
             after, before = z_pair([out[2, x - 1, ys, pl.ds(j * L, L)] for j in range(nj)], lane)
@@ -529,10 +584,33 @@
                 middle = (out_s[x - 1, ys, pl.ds(j * L, L)] - source) * (1.0 / 6.0)
                 field[0, x, j, pl.ds(PAD + y, 8), :] = middle
                 out_s[x - 1, ys, pl.ds(j * L, L)] = source
-        pack(ysm, (), field, (0, x), x)
-
-    x_start(2)
-    y_start("mid_lo", "mid_hi")
+
+    x_wait_recv(MID)
+    y_wait_recv(1)
+
+    def add_middle(direction, kept, j):
+        field[0, kept, j, rows, :] += (1.0 / 6.0) * x_in[MID, direction, j]
+
+    x_faces(add_middle)
+
+    def add_middle_rows(direction, y, sign, x, j):
+        field[0, x, j, pl.ds(PAD + y, 1), :] += (1.0 / 6.0) * y_in[0, direction, x - 1, pl.ds(j, 1)]
+
+    y_rows(far_edges, add_middle_rows)
+
+    @pl.loop(0, nj)
+    def _(j):
+        for direction, kept, sign in ((0, 1, -0.5), (1, nx, 0.5)):
+            x_out[2, direction, j] = field[0, kept, j, rows, :] + sign * push0[kept, j]
+
+    x_start(SET)
+
+    def pack_settled(direction, y, sign, x, j):
+        at = pl.ds(PAD + y, 1)
+        y_out[1, direction, x - 1, pl.ds(j, 1)] = field[0, x, j, at, :] + (0.5 * sign) * push1[x - 1, j, at, :]
+
+    y_rows(edges, pack_settled)
+    y_start(2)
 
     @pl.loop(1, n_sector)
     def _(d):
@@ -549,19 +627,10 @@
     def _(d):
         slab_copy(d).start()
 
-    y_wait_recv("mid_in")
-
-    @pl.loop(0, nx)
-    def _(i):
-        x = plane_of(i)
-
-        @pl.when(i == nx - 2)
-        def _():
-            y_start("set_in")
-            y_wait_recv("mid_lo", "mid_hi")
-            x_wait_recv(2)
-
-        unpack(yrm, (), field, (0, x), x)
+    x_wait_send(V1)
+
+    @pl.loop(1, nx + 1)
+    def _(x):
         for y in range(0, ny, 8):
             ys = pl.ds(y, 8)
             here = pl.ds(PAD + y, 8)
@@ -574,36 +643,58 @@
                 )
                 settled = (total - out_s[x - 1, ys, pl.ds(j * L, L)]) * (1.0 / 6.0)
                 field[1, x, j, here, :] = settled
-                out_s[x - 1, ys, pl.ds(j * L, L)] = settled
-        pack(yss, (), field, (1, x), x)
-
-    x_start(3)
-    y_start("set_lo", "set_hi")
-
-    y_wait_recv("set_in")
-
-    @pl.loop(0, nx)
-    def _(i):
-        x = plane_of(i)
-
-        @pl.when(i == nx - 2)
-        def _():
-            y_wait_recv("set_lo", "set_hi")
-            x_wait_recv(3)
-
-        unpack(yrs, (), field, (1, x), x)
+
+    x_wait_recv(SET)
+    y_wait_recv(2)
+
+    def add_settled(direction, kept, j):
+        field[1, kept, j, rows, :] += (1.0 / 6.0) * x_in[SET, direction, j]
+
+    x_faces(add_settled)
+
+    def add_settled_rows(direction, y, sign, x, j):
+        field[1, x, j, pl.ds(PAD + y, 1), :] += (1.0 / 6.0) * y_in[1, direction, x - 1, pl.ds(j, 1)]
+
+    y_rows(far_edges, add_settled_rows)
+    x_start(COR)
+
+    def pack_corrected(direction, y, sign, x, j):
+        y_out[2, direction, x - 1, pl.ds(j, 1)] = field[1, x, j, pl.ds(PAD + y, 1), :]
+
+    y_rows(edges, pack_corrected)
+    y_start(3)
+
+    @pl.loop(1, nx + 1)
+    def _(x):
         for y in range(0, ny, 8):
             ys = pl.ds(y, 8)
             here = pl.ds(PAD + y, 8)
-            after, before = z_pair([field[1, x, j, here, :] for j in range(nj)], lane)
+            centre = [field[1, x, j, here, :] for j in range(nj)]
+            after, before = z_pair(centre, lane)
             for j in range(nj):
                 zs = pl.ds(j * L, L)
+                out_s[x - 1, ys, zs] = centre[j]
                 out[0, x - 1, ys, zs] = push0[x, j, ys, :] - 0.5 * (field[1, x + 1, j, here, :] - field[1, x - 1, j, here, :])
                 out[1, x - 1, ys, zs] = push1[x - 1, j, here, :] - 0.5 * (
                     field[1, x, j, pl.ds(PAD + y + 1, 8), :] - field[1, x, j, pl.ds(PAD + y - 1, 8), :]
                 )
                 out[2, x - 1, ys, zs] = out[2, x - 1, ys, zs] - 0.5 * (after[j] - before[j])
 
+    x_wait_recv(COR)
+    for direction, there, kept, sign in ((0, has_right, nx, -0.5), (1, has_left, 1, 0.5)):
+
+        @pl.when(there)
+        def _():
+            for j in range(nj):
+                out[0, kept - 1, :, pl.ds(j * L, L)] += sign * x_in[COR, direction, j]
+
+    y_wait_recv(3)
+
+    def add_corrected_rows(direction, y, sign, x, j):
+        out[1, x - 1, pl.ds(y, 1), pl.ds(j * L, L)] += (0.5 * sign) * y_in[2, direction, x - 1, pl.ds(j, 1)]
+
+    y_rows(far_edges, add_corrected_rows)
+
     @pl.loop(1, n_slab)
     def _(d):
         slab_copy(d).wait_recv()
@@ -613,19 +704,16 @@
         final = final + slab_recv[d]
     loads[...] = final[0:2, 0:sec_dev]
 
-    for stage in range(1, 4):
+    for stage in (W0, V2, MID, SET, COR):
         x_wait_send(stage)
-    for copies in y_all.values():
+    for copies in y_all:
         for c in copies:
             c.wait_send()
 
-    @pl.loop(1, half)
-    def _(k):
+    for k in range(7):
         table_copy(k).wait_send()
-
-    @pl.loop(0, half)
-    def _(k):
-        twin_copy(k).wait_send()
+    for c in twins:
+        c.wait_send()
 
     @pl.loop(1, n_sector)
     def _(d):
@@ -660,7 +748,8 @@
             pltpu.VMEM((4, nx + 2, nj, tall, L), F32),
             pltpu.VMEM((nx + 2, nj, ny, L), F32),
             pltpu.VMEM((nx, nj, tall, L), F32),
-            pltpu.VMEM((2, nj, ny, L), F32),
+            pltpu.VMEM((3, 2, nj, ny, L), F32),
+            pltpu.VMEM((6, 2, nj, ny, L), F32),
             pltpu.SMEM((1, slots), jnp.int32),
             pltpu.SMEM((1, slots), jnp.int32),
             pltpu.SMEM((1, slots), jnp.int32),
@@ -677,24 +766,20 @@
             pltpu.VMEM((slots, L), F32),
             pltpu.VMEM((slots, L), F32),
             pltpu.VMEM((2, 2, slots, nz), BF16),
-            pltpu.VMEM((2, 4, nx, 8, L), F32),
-            pltpu.VMEM((2, 4, nx, 8, L), F32),
-            pltpu.VMEM((2, nx, 8, L), F32),
-            pltpu.VMEM((2, nx, 8, L), F32),
-            pltpu.VMEM((2, nx, 8, L), F32),
-            pltpu.VMEM((2, nx, 8, L), F32),
-            pltpu.VMEM((2, nx, 8, L), F32),
-            pltpu.VMEM((2, nx, 8, L), F32),
+            pltpu.VMEM((2, 3, nx, 8, L), F32),
+            pltpu.VMEM((2, 3, nx, 8, L), F32),
+            pltpu.VMEM((3, 2, nx, 8, L), F32),
+            pltpu.VMEM((3, 2, nx, 8, L), F32),
             pltpu.VMEM((half, 8, L), F32),
             pltpu.VMEM((n_sector, 8, L), F32),
             pltpu.VMEM((8, L), F32),
             pltpu.VMEM((n_slab, 8, L), F32),
-            dma((2, nx // 4, nj)),
+            dma((2, 4, nj)),
             dma((bins // L,)),
+            dma((6, 2)),
+            dma((6, 2)),
             dma((4, 2)),
             dma((4, 2)),
-            dma((8, 2)),
-            dma((8, 2)),
             dma((half,)),
             dma((half,)),
             dma((half,)),

time: 95.5 us -> 73.4 us (0.77)
  the two profiles are of different devices: /device:TPU:30 before, /device:TPU:0 now
where the time goes in v2:
time: 73.4 us; the launch traced here: 72.9 us
  Pallas kernels  65.7 us (90%)
  local copies, waits for them, and re-layouts  5.97 us (8%)
  between operations  1.29 us (2%)
    pallas_call x1, Pallas kernels, on_device(): pl.pallas_call(functools.partial(kernel, n_slab, n_sector), out_shape=(pl...  65.7 us
    unnamed x3, local copies, waits for them, and re-layouts  5.97 us

profile of v2, /device:TPU:0, one launch (start us, length us, event | category | flops | bytes accessed | tf_op | source)
XLA Modules:
  0.0 72.9 jit_solution(13704006259315967951)
XLA Ops:
  1.3 65.7 %shard_map.103 = (f32[3,16,64,768]{3,2,1,0:T(8,128)S(1)}, f32[16,64,768]{2,1,0:T(8,128)S(1)}, f32[2,64]{1,0:T(2,128)S(1)}) custom-call(f32[3,16,64,768]{3,2,1,0:T(8,128)} %vel.1, f32[16,64,768]{2,1,0:T(8,128)} %pre.1, s32[1,512]{1,0:T(1,128)} %cell_h.1, s32[1,512]{1,0:T(1,128)} %bitcast.1, s32[1,512]{1,0:T(1,128)} %section_h.1, f32[2,64,256]{2,1,0:T(8,128)} %polar.1, ...), custom_call_target="tpu_custom_call" | custom-call | tf_op jit(solution)/shard_map/pallas_call | solution.py:738
  67.0 3.7 %copy.14 = f32[3,16,64,768]{3,2,1,0:T(8,128)} copy(f32[3,16,64,768]{3,2,1,0:T(8,128)S(1)} %get-tuple-element.3) | data formatting | bytes 18874368
  70.7 1.7 %copy.15 = f32[16,64,768]{2,1,0:T(8,128)} copy(f32[16,64,768]{2,1,0:T(8,128)S(1)} %get-tuple-element.4) | data formatting | bytes 6291456
  72.4 0.6 copy.17

commit v3 on v2

--- a/solution.py
+++ b/solution.py
@@ -170,58 +170,51 @@
         buffer[...] = jnp.zeros(buffer.shape, F32)
     W0, V1, V2, MID, SET, COR = range(6)
 
-    def x_copy(stage, direction):
+    halves = (0, 1)
+    deep = nj // 2
+
+    def x_copy(stage, direction, h):
         kept = 1 if direction == 0 else nx
+        js = pl.ds(h * deep, deep)
         if stage in (V1, V2):
-            src = field.at[stage, kept, :, rows, :]
+            src = field.at[stage, kept, js, rows, :]
         elif stage == COR:
-            src = field.at[1, kept, :, rows, :]
+            src = field.at[1, kept, js, rows, :]
         else:
-            src = x_out.at[{W0: 0, MID: 1, SET: 2}[stage], direction]
+            src = x_out.at[{W0: 0, MID: 1, SET: 2}[stage], direction, js]
         return pltpu.make_async_remote_copy(
             src_ref=src,
-            dst_ref=x_in.at[stage, direction],
-            send_sem=x_send.at[stage, direction],
-            recv_sem=x_recv.at[stage, direction],
+            dst_ref=x_in.at[stage, direction, js],
+            send_sem=x_send.at[stage, direction, h],
+            recv_sem=x_recv.at[stage, direction, h],
             device_id=(sl - 1 if direction == 0 else sl + 1, se),
             device_id_type=MESH,
         )
 
-    def x_faces(body):
+    def x_faces(body, h=None):
         for direction, there, kept in ((0, has_right, nx), (1, has_left, 1)):
 
             @pl.when(there)
             def _():
-                @pl.loop(0, nj)
-                def _(j):
+                for j in range(nj) if h is None else range(h * deep, (h + 1) * deep):
                     body(direction, kept, j)
 
-    def x_start(stage):
-        @pl.when(has_left)
-        def _():
-            x_copy(stage, 0).start()
-
-        @pl.when(has_right)
-        def _():
-            x_copy(stage, 1).start()
-
-    def x_wait_recv(stage):
-        @pl.when(has_right)
-        def _():
-            x_copy(stage, 0).wait_recv()
-
-        @pl.when(has_left)
-        def _():
-            x_copy(stage, 1).wait_recv()
+    def x_each(act, sending, stage, parts):
+        for h in parts:
+            for direction, there in ((0, has_left if sending else has_right), (1, has_right if sending else has_left)):
+
+                @pl.when(there)
+                def _():
+                    act(x_copy(stage, direction, h))
+
+    def x_start(stage, parts=halves):
+        x_each(lambda c: c.start(), True, stage, parts)
+
+    def x_wait_recv(stage, parts=halves):
+        x_each(lambda c: c.wait_recv(), False, stage, parts)
 
     def x_wait_send(stage):
-        @pl.when(has_left)
-        def _():
-            x_copy(stage, 0).wait_send()
-
-        @pl.when(has_right)
-        def _():
-            x_copy(stage, 1).wait_send()
+        x_each(lambda c: c.wait_send(), True, stage, halves)
 
     below = (sl, lax.rem(se + n_sector - 1, n_sector))
     above = (sl, lax.rem(se + 1, n_sector))
@@ -271,7 +264,7 @@
     relay_from = down + (up - down) * core
     relay_to = up + (down - up) * core
 
-    def table_copy(k):
+    def table_copy(k, h):
         block, target = (
             ((0, 0), (1, 0)),
             ((0, 0), (0, up)),
@@ -282,27 +275,27 @@
             ((1, relay_from), (0, relay_to)),
         )[k]
         return pltpu.make_async_remote_copy(
-            src_ref=table.at[at_step(*block)],
-            dst_ref=table.at[at_step(*block)],
-            send_sem=t_send.at[k],
-            recv_sem=t_recv.at[k],
+            src_ref=table.at[at_step(*block), h],
+            dst_ref=table.at[at_step(*block), h],
+            send_sem=t_send.at[k, h],
+            recv_sem=t_recv.at[k, h],
             device_id=(sl, at_step(*target)),
             device_id_type=MESH,
         )
 
     twin = se + 1 - 2 * core
 
-    def twin_copy(dy, dz):
+    def twin_copy(dy, dz, h):
         return pltpu.make_async_remote_copy(
-            src_ref=table.at[at_step(dy, dz)],
-            dst_ref=table.at[at_step(dy, dz)],
-            send_sem=w_send.at[dy * tall_z + dz],
-            recv_sem=w_recv.at[dy * tall_z + dz],
+            src_ref=table.at[at_step(dy, dz), h],
+            dst_ref=table.at[at_step(dy, dz), h],
+            send_sem=w_send.at[dy * tall_z + dz, h],
+            recv_sem=w_recv.at[dy * tall_z + dz, h],
             device_id=(sl, twin),
             device_id_type=MESH,
         )
 
-    twins = [twin_copy(dy, dz) for dy in range(2) for dz in range(tall_z)]
+    twins = [twin_copy(dy, dz, h) for dy in range(2) for dz in range(tall_z) for h in range(2)]
 
     half = n_sector // 2
 
@@ -324,9 +317,10 @@
     x_start(V1)
     for c in polar_copies:
         c.wait()
-    for k in range(3):
-        table_copy(k).start()
-    twin_copy(0, 0).start()
+    for h in range(2):
+        for k in range(3):
+            table_copy(k, h).start()
+        twin_copy(0, 0, h).start()
     wait_part(2)
     wait_part(3)
 
@@ -344,20 +338,22 @@
 
     @pl.loop(1, nx + 1)
     def _(x):
-        @pl.when(x == nx // 2 + 1)
-        def _():
-            table_copy(1).wait_recv()
-            table_copy(2).wait_recv()
-            table_copy(5).start()
-            twin_copy(0, up).start()
-            twin_copy(0, down).start()
-
-        @pl.when(x == nx // 2 + 4)
-        def _():
-            table_copy(0).wait_recv()
-            table_copy(3).start()
-            table_copy(4).start()
-            twin_copy(1, 0).start()
+        for h in range(2):
+
+            @pl.when(x == nx // 2 - 1 + 4 * h)
+            def _():
+                table_copy(1, h).wait_recv()
+                table_copy(2, h).wait_recv()
+                table_copy(5, h).start()
+                twin_copy(0, up, h).start()
+                twin_copy(0, down, h).start()
+
+            @pl.when(x == nx // 2 + 1 + 5 * h)
+            def _():
+                table_copy(0, h).wait_recv()
+                table_copy(3, h).start()
+                table_copy(4, h).start()
+                twin_copy(1, 0, h).start()
 
         for y in range(0, ny, 8):
             here = pl.ds(PAD + y, 8)
@@ -391,13 +387,14 @@
                     else:
                         out[2, x - 1, pl.ds(y, 8), pl.ds(j * L, L)] = value
 
-    table_copy(5).wait_recv()
-    twin_copy(0, 2).start()
-    table_copy(3).wait_recv()
-    table_copy(4).wait_recv()
-    table_copy(6).start()
-    twin_copy(1, up).start()
-    twin_copy(1, down).start()
+    for h in range(2):
+        table_copy(5, h).wait_recv()
+        twin_copy(0, 2, h).start()
+        table_copy(3, h).wait_recv()
+        table_copy(4, h).wait_recv()
+        table_copy(6, h).start()
+        twin_copy(1, up, h).start()
+        twin_copy(1, down, h).start()
     x_wait_recv(W0)
     x_wait_recv(V1)
     x_start(V2)
@@ -417,7 +414,7 @@
 
     y_rows(far_edges, add_first_rows)
 
-    @pl.loop(0, slots, unroll=4)
+    @pl.loop(0, slots, unroll=16)
     def _(s):
         cell = cell_s[0, s]
         xy = ((cell >> 8) * 21846) >> 16
@@ -429,12 +426,13 @@
         row0[at, :] = push0[x + 1, j, pl.ds(y, 1), :]
         row1[at, :] = push1[x, j, pl.ds(y + PAD, 1), :]
 
-    table_copy(6).wait_recv()
-    twin_copy(1, 2).start()
+    for h in range(2):
+        table_copy(6, h).wait_recv()
+        twin_copy(1, 2, h).start()
     for c in twins:
         c.wait_recv()
 
-    @pl.loop(0, slots, unroll=4)
+    @pl.loop(0, slots, unroll=16)
     def _(s):
         owner = owner_s[0, s]
         section = section_s[0, s]
@@ -491,10 +489,9 @@
             high = force.astype(BF16).astype(F32)
             rhs[c, 0, at, :] = jnp.where(mask, high, 0.0).astype(BF16)
             rhs[c, 1, at, :] = jnp.where(mask, force - high, 0.0).astype(BF16)
-        for pair in range(half):
-            chosen = lanes == whole - float(pair * L)
-            load_send[pair, 0:1, :] += jnp.sum(jnp.where(chosen, thrust, 0.0), axis=0, keepdims=True)
-            load_send[pair, 1:2, :] += jnp.sum(jnp.where(chosen, torque, 0.0), axis=0, keepdims=True)
+        geo0[at, 0:1] = thrust
+        geo1[at, 0:1] = torque
+        row0[at, 0:1] = whole
 
     def load_copy(d):
         peer = lax.rem(se + d, n_sector)
@@ -521,21 +518,22 @@
     high_rows = lax.broadcasted_iota(I32, (chunk * ny, slots), 0)
     xy_all = xy_of(cell_v[...])
 
+    def put_back(c, m):
+        chosen = jnp.where(high_rows == xy_all - m * (chunk * ny), 1.0, 0.0).astype(BF16)
+        total = jnp.dot(chosen, rhs[c, 0], preferred_element_type=F32) + jnp.dot(
+            chosen, rhs[c, 1], preferred_element_type=F32
+        )
+        for k in range(chunk):
+            for j in range(nj):
+                piece = total[k * ny : (k + 1) * ny, j * L : (j + 1) * L]
+                if c == 0:
+                    push0[1 + m * chunk + k, j] += piece
+                else:
+                    push1[m * chunk + k, j, rows, :] += piece
+
     @pl.loop(0, nx // chunk)
     def _(i):
-        m = jnp.where(i == 0, 0, jnp.where(i == 1, nx // chunk - 1, i - 1))
-        chosen = jnp.where(high_rows == xy_all - m * (chunk * ny), 1.0, 0.0).astype(BF16)
-        for c in range(2):
-            total = jnp.dot(chosen, rhs[c, 0], preferred_element_type=F32) + jnp.dot(
-                chosen, rhs[c, 1], preferred_element_type=F32
-            )
-            for k in range(chunk):
-                for j in range(nj):
-                    piece = total[k * ny : (k + 1) * ny, j * L : (j + 1) * L]
-                    if c == 0:
-                        push0[1 + m * chunk + k, j] += piece
-                    else:
-                        push1[m * chunk + k, j, rows, :] += piece
+        put_back(0, jnp.where(i == 0, 0, jnp.where(i == 1, nx // chunk - 1, i - 1)))
 
         @pl.when(i == 1)
         def _():
@@ -546,6 +544,10 @@
 
             x_start(MID)
 
+    @pl.loop(0, nx // chunk)
+    def _(i):
+        put_back(1, i)
+
     def pack_middle(direction, y, sign, x, j):
         at = pl.ds(PAD + y, 1)
         y_out[0, direction, x - 1, pl.ds(j, 1)] = field[3, x, j, at, :] + (0.5 * sign) * push1[x - 1, j, at, :]
@@ -553,20 +555,10 @@
     y_rows(edges, pack_middle)
     y_start(1)
 
-    @pl.loop(1, n_sector)
-    def _(d):
-        load_copy(d).start()
-
-    load_recv[se] = load_send[se // 2]
-
     x_wait_recv(V2)
 
     def add_depth(direction, kept, j):
-        for k in range(nj):
-
-            @pl.when(j == k)
-            def _():
-                out[2, kept - 1, :, pl.ds(k * L, L)] += 0.1 * x_in[V2, direction, k]
+        out[2, kept - 1, :, pl.ds(j * L, L)] += 0.1 * x_in[V2, direction, j]
 
     x_faces(add_depth)
 
@@ -585,25 +577,23 @@
                 field[0, x, j, pl.ds(PAD + y, 8), :] = middle
                 out_s[x - 1, ys, pl.ds(j * L, L)] = source
 
-    x_wait_recv(MID)
     y_wait_recv(1)
+
+    def add_middle_rows(direction, y, sign, x, j):
+        field[0, x, j, pl.ds(PAD + y, 1), :] += (1.0 / 6.0) * y_in[0, direction, x - 1, pl.ds(j, 1)]
+
+    y_rows(far_edges, add_middle_rows)
 
     def add_middle(direction, kept, j):
         field[0, kept, j, rows, :] += (1.0 / 6.0) * x_in[MID, direction, j]
 
-    x_faces(add_middle)
-
-    def add_middle_rows(direction, y, sign, x, j):
-        field[0, x, j, pl.ds(PAD + y, 1), :] += (1.0 / 6.0) * y_in[0, direction, x - 1, pl.ds(j, 1)]
-
-    y_rows(far_edges, add_middle_rows)
-
-    @pl.loop(0, nj)
-    def _(j):
-        for direction, kept, sign in ((0, 1, -0.5), (1, nx, 0.5)):
-            x_out[2, direction, j] = field[0, kept, j, rows, :] + sign * push0[kept, j]
-
-    x_start(SET)
+    for h in halves:
+        x_wait_recv(MID, (h,))
+        x_faces(add_middle, h)
+        for j in range(h * deep, (h + 1) * deep):
+            for direction, kept, sign in ((0, 1, -0.5), (1, nx, 0.5)):
+                x_out[2, direction, j] = field[0, kept, j, rows, :] + sign * push0[kept, j]
+        x_start(SET, (h,))
 
     def pack_settled(direction, y, sign, x, j):
         at = pl.ds(PAD + y, 1)
@@ -612,20 +602,21 @@
     y_rows(edges, pack_settled)
     y_start(2)
 
+    for pair in range(half):
+        thrust_sum = torque_sum = 0.0
+        for g in range(slots // L):
+            at = pl.ds(g * L, L)
+            chosen = lanes == row0[at, 0:1] - float(pair * L)
+            thrust_sum = thrust_sum + jnp.where(chosen, geo0[at, 0:1], 0.0)
+            torque_sum = torque_sum + jnp.where(chosen, geo1[at, 0:1], 0.0)
+        load_send[pair, 0:1, :] = jnp.sum(thrust_sum, axis=0, keepdims=True)
+        load_send[pair, 1:2, :] = jnp.sum(torque_sum, axis=0, keepdims=True)
+
     @pl.loop(1, n_sector)
     def _(d):
-        load_copy(d).wait_recv()
-
-    mine = load_recv[0]
-    for d in range(1, n_sector):
-        mine = mine + load_recv[d]
-    mine = jnp.where(lax.rem(se, 2) == 1, pltpu.roll(mine, L // 2, 1), mine)
-    slab_send[...] = mine
-    slab_recv[sl] = mine
-
-    @pl.loop(1, n_slab)
-    def _(d):
-        slab_copy(d).start()
+        load_copy(d).start()
+
+    load_recv[se] = load_send[se // 2]
 
     x_wait_send(V1)
 
@@ -644,25 +635,41 @@
                 settled = (total - out_s[x - 1, ys, pl.ds(j * L, L)]) * (1.0 / 6.0)
                 field[1, x, j, here, :] = settled
 
-    x_wait_recv(SET)
     y_wait_recv(2)
+
+    def add_settled_rows(direction, y, sign, x, j):
+        field[1, x, j, pl.ds(PAD + y, 1), :] += (1.0 / 6.0) * y_in[1, direction, x - 1, pl.ds(j, 1)]
+
+    y_rows(far_edges, add_settled_rows)
 
     def add_settled(direction, kept, j):
         field[1, kept, j, rows, :] += (1.0 / 6.0) * x_in[SET, direction, j]
 
-    x_faces(add_settled)
-
-    def add_settled_rows(direction, y, sign, x, j):
-        field[1, x, j, pl.ds(PAD + y, 1), :] += (1.0 / 6.0) * y_in[1, direction, x - 1, pl.ds(j, 1)]
-
-    y_rows(far_edges, add_settled_rows)
-    x_start(COR)
+    for h in halves:
+        x_wait_recv(SET, (h,))
+        x_faces(add_settled, h)
+        x_start(COR, (h,))
 
     def pack_corrected(direction, y, sign, x, j):
         y_out[2, direction, x - 1, pl.ds(j, 1)] = field[1, x, j, pl.ds(PAD + y, 1), :]
 
     y_rows(edges, pack_corrected)
     y_start(3)
+
+    @pl.loop(1, n_sector)
+    def _(d):
+        load_copy(d).wait_recv()
+
+    mine = load_recv[0]
+    for d in range(1, n_sector):
+        mine = mine + load_recv[d]
+    mine = jnp.where(lax.rem(se, 2) == 1, pltpu.roll(mine, L // 2, 1), mine)
+    slab_send[...] = mine
+    slab_recv[sl] = mine
+
+    @pl.loop(1, n_slab)
+    def _(d):
+        slab_copy(d).start()
 
     @pl.loop(1, nx + 1)
     def _(x):
@@ -680,20 +687,19 @@
                 )
                 out[2, x - 1, ys, zs] = out[2, x - 1, ys, zs] - 0.5 * (after[j] - before[j])
 
-    x_wait_recv(COR)
-    for direction, there, kept, sign in ((0, has_right, nx, -0.5), (1, has_left, 1, 0.5)):
-
-        @pl.when(there)
-        def _():
-            for j in range(nj):
-                out[0, kept - 1, :, pl.ds(j * L, L)] += sign * x_in[COR, direction, j]
-
     y_wait_recv(3)
 
     def add_corrected_rows(direction, y, sign, x, j):
         out[1, x - 1, pl.ds(y, 1), pl.ds(j * L, L)] += (0.5 * sign) * y_in[2, direction, x - 1, pl.ds(j, 1)]
 
     y_rows(far_edges, add_corrected_rows)
+
+    def add_corrected(direction, kept, j):
+        out[0, kept - 1, :, pl.ds(j * L, L)] += (-0.5 if direction == 0 else 0.5) * x_in[COR, direction, j]
+
+    for h in halves:
+        x_wait_recv(COR, (h,))
+        x_faces(add_corrected, h)
 
     @pl.loop(1, n_slab)
     def _(d):
@@ -711,7 +717,8 @@
             c.wait_send()
 
     for k in range(7):
-        table_copy(k).wait_send()
+        for h in range(2):
+            table_copy(k, h).wait_send()
     for c in twins:
         c.wait_send()
 
@@ -776,14 +783,14 @@
             pltpu.VMEM((n_slab, 8, L), F32),
             dma((2, 4, nj)),
             dma((bins // L,)),
-            dma((6, 2)),
-            dma((6, 2)),
+            dma((6, 2, 2)),
+            dma((6, 2, 2)),
             dma((4, 2)),
             dma((4, 2)),
-            dma((half,)),
-            dma((half,)),
-            dma((half,)),
-            dma((half,)),
+            dma((half, 2)),
+            dma((half, 2)),
+            dma((half, 2)),
+            dma((half, 2)),
             dma((n_sector,)),
             dma((n_sector,)),
             dma((n_slab,)),

time: 73.4 us -> 70.1 us (0.955)
  Pallas kernels: 65.7 us -> 62.6 us
    pallas_call x1, Pallas kernels: 65.7 us -> 62.6 us  [on_device(): pl.pallas_call(functools.partial(kernel, n_slab, n_sector), out_shape=(pl...]
where the time goes in v3:
time: 70.1 us; the launch traced here: 69.9 us
  Pallas kernels  62.6 us (89%)
  local copies, waits for them, and re-layouts  5.97 us (9%)
  between operations  1.29 us (2%)
    pallas_call x1, Pallas kernels, on_device(): pl.pallas_call(functools.partial(kernel, n_slab, n_sector), out_shape=(pl...  62.6 us
    unnamed x3, local copies, waits for them, and re-layouts  5.97 us

profile of v3, /device:TPU:0, one launch (start us, length us, event | category | flops | bytes accessed | tf_op | source)
XLA Modules:
  0.0 69.9 jit_solution(14558912845006747992)
XLA Ops:
  1.3 62.6 %shard_map.103 = (f32[3,16,64,768]{3,2,1,0:T(8,128)S(1)}, f32[16,64,768]{2,1,0:T(8,128)S(1)}, f32[2,64]{1,0:T(2,128)S(1)}) custom-call(f32[3,16,64,768]{3,2,1,0:T(8,128)} %vel.1, f32[16,64,768]{2,1,0:T(8,128)} %pre.1, s32[1,512]{1,0:T(1,128)} %cell_h.1, s32[1,512]{1,0:T(1,128)} %bitcast.1, s32[1,512]{1,0:T(1,128)} %section_h.1, f32[2,64,256]{2,1,0:T(8,128)} %polar.1, ...), custom_call_target="tpu_custom_call" | custom-call | tf_op jit(solution)/shard_map/pallas_call | solution.py:745
  63.9 3.7 %copy.14 = f32[3,16,64,768]{3,2,1,0:T(8,128)} copy(f32[3,16,64,768]{3,2,1,0:T(8,128)S(1)} %get-tuple-element.3) | data formatting | bytes 18874368
  67.6 1.7 %copy.15 = f32[16,64,768]{2,1,0:T(8,128)} copy(f32[16,64,768]{2,1,0:T(8,128)S(1)} %get-tuple-element.4) | data formatting | bytes 6291456
  69.3 0.6 copy.17

commit v4 on v3

--- a/solution.py
+++ b/solution.py
@@ -426,23 +426,6 @@
         row0[at, :] = push0[x + 1, j, pl.ds(y, 1), :]
         row1[at, :] = push1[x, j, pl.ds(y + PAD, 1), :]
 
-    for h in range(2):
-        table_copy(6, h).wait_recv()
-        twin_copy(1, 2, h).start()
-    for c in twins:
-        c.wait_recv()
-
-    @pl.loop(0, slots, unroll=16)
-    def _(s):
-        owner = owner_s[0, s]
-        section = section_s[0, s]
-        at = pl.ds(s, 1)
-        for b in range(bins // L):
-            lift_rows[b, at, :] = table[owner, 0, b, pl.ds(section, 1), :]
-            drag_rows[b, at, :] = table[owner, 1, b, pl.ds(section, 1), :]
-        geo0[at, :] = table[owner, 0, 0, pl.ds(sec_dev, 1), :]
-        geo1[at, :] = table[owner, 1, 0, pl.ds(sec_dev, 1), :]
-
     diagonal = lax.broadcasted_iota(I32, (L, L), 0) == lax.broadcasted_iota(I32, (L, L), 1)
     lanes = lax.broadcasted_iota(I32, (L, L), 1).astype(F32)
     z_ids = lax.broadcasted_iota(I32, (L, nz), 1).astype(F32)
@@ -458,6 +441,7 @@
     def xy_of(cell):
         return (((cell >> 8).astype(F32) + 0.5) * (1.0 / 3.0)).astype(I32)
 
+    flow = []
     for g in range(slots // L):
         at = pl.ds(g * L, L)
         cell = cell_v[0:1, at]
@@ -469,9 +453,33 @@
         radius = 0.25 + 0.75 * (z_col + 0.5) / nz
         a = 1.0 + picked(row0[at, :], lane_col)
         t = 10.0 * radius + picked(row1[at, :], lane_col)
+        speed = jnp.where(places + g * L < used, 0.5 * jnp.sqrt(a * a + t * t), 0.0)
+        row0[at, 0:1] = whole
+        flow.append((z_col, section, radius, a, t, jnp.arctan2(a, t), speed))
+
+    for h in range(2):
+        table_copy(6, h).wait_recv()
+        twin_copy(1, 2, h).start()
+    for c in twins:
+        c.wait_recv()
+
+    @pl.loop(0, slots, unroll=16)
+    def _(s):
+        owner = owner_s[0, s]
+        section = section_s[0, s]
+        at = pl.ds(s, 1)
+        for b in range(bins // L):
+            lift_rows[b, at, :] = table[owner, 0, b, pl.ds(section, 1), :]
+            drag_rows[b, at, :] = table[owner, 1, b, pl.ds(section, 1), :]
+        geo0[at, :] = table[owner, 0, 0, pl.ds(sec_dev, 1), :]
+        geo1[at, :] = table[owner, 1, 0, pl.ds(sec_dev, 1), :]
+
+    for g in range(slots // L):
+        at = pl.ds(g * L, L)
+        z_col, section, radius, a, t, angle, speed = flow[g]
         chord = picked(geo0[at, :], section)
         twist = picked(geo1[at, :], section)
-        position = (jnp.arctan2(a, t) - twist + 2.0) * ((bins - 1) / 4.0)
+        position = (angle - twist + 2.0) * ((bins - 1) / 4.0)
         lift, drag = 0.0, 0.0
         for b in range(bins // L):
             weight = jnp.maximum(0.0, 1.0 - jnp.abs(position - (lanes + float(b * L))))
@@ -479,19 +487,16 @@
             drag = drag + drag_rows[b, at, :] * weight
         lift = jnp.sum(lift, axis=1, keepdims=True)
         drag = jnp.sum(drag, axis=1, keepdims=True)
-        scale = 0.5 * chord * jnp.sqrt(a * a + t * t)
-        active = places + g * L < used
-        thrust = jnp.where(active, scale * (lift * t - drag * a), 0.0)
-        swirl = jnp.where(active, scale * (lift * a + drag * t), 0.0)
-        torque = swirl * radius
+        scale = speed * chord
+        thrust = scale * (lift * t - drag * a)
+        swirl = scale * (lift * a + drag * t)
         mask = z_ids == z_col
         for c, force in ((0, 0.2 * thrust), (1, 0.2 * swirl)):
             high = force.astype(BF16).astype(F32)
             rhs[c, 0, at, :] = jnp.where(mask, high, 0.0).astype(BF16)
             rhs[c, 1, at, :] = jnp.where(mask, force - high, 0.0).astype(BF16)
         geo0[at, 0:1] = thrust
-        geo1[at, 0:1] = torque
-        row0[at, 0:1] = whole
+        geo1[at, 0:1] = swirl * radius
 
     def load_copy(d):
         peer = lax.rem(se + d, n_sector)
@@ -729,6 +734,15 @@
     @pl.loop(1, n_slab)
     def _(d):
         slab_copy(d).wait_send()
+
+
+def write_back(fields, settled, loads, fields_out, settled_out, loads_out, sems):
+    pairs = [(fields.at[k], fields_out.at[k]) for k in range(3)] + [(settled, settled_out), (loads, loads_out)]
+    copies = [pltpu.make_async_copy(src, dst, sems.at[k]) for k, (src, dst) in enumerate(pairs)]
+    for c in copies:
+        c.start()
+    for c in copies:
+        c.wait()
 
 
 def on_device(n_slab, n_sector, velocity, pressure, disk_cell, disk_count, disk_owner, disk_section, polar, geometry):
@@ -747,7 +761,7 @@
         out_shape=(
             pltpu.VMEM((3, nx, ny, nz), F32),
             pltpu.VMEM((nx, ny, nz), F32),
-            jax.ShapeDtypeStruct((2, sec_dev), F32),
+            pltpu.VMEM((2, sec_dev), F32),
         ),
         in_specs=[hbm] * 7 + [pl.BlockSpec(memory_space=pltpu.SMEM)],
         out_specs=(vmem, vmem, vmem),
@@ -806,7 +820,18 @@
         ),
         disk_count,
     )
-    return corrected, settled, loads
+    return pl.pallas_call(
+        write_back,
+        out_shape=(
+            jax.ShapeDtypeStruct((3, nx, ny, nz), F32),
+            jax.ShapeDtypeStruct((nx, ny, nz), F32),
+            jax.ShapeDtypeStruct((2, sec_dev), F32),
+        ),
+        in_specs=[vmem] * 3,
+        out_specs=(hbm,) * 3,
+        scratch_shapes=[dma((5,))],
+        compiler_params=pltpu.CompilerParams(vmem_limit_bytes=1024 * 1024),
+    )(*(pltpu.with_memory_space_constraint(array, pltpu.VMEM) for array in (corrected, settled, loads)))
 
 
 def solution(mesh):

time: 70.1 us -> 68.6 us (0.979)
  local copies, waits for them, and re-layouts: 5.97 us -> 0 us
  Pallas kernels: 62.6 us -> 67 us
    unnamed x3 -> x0, local copies, waits for them, and re-layouts: 5.97 us -> none
    pallas_call x0 -> x1, Pallas kernels: none -> 4.73 us  [on_device(): pl.pallas_call(write_back, out_shape=(jax.ShapeDtypeStruct((3, nx, ny, nz...]
where the time goes in v4:
time: 68.6 us; the launch traced here: 68.2 us
  Pallas kernels  67 us (98%)
  between operations  1.29 us (2%)
    pallas_call x1, Pallas kernels, on_device(): pl.pallas_call(functools.partial(kernel, n_slab, n_sector), out_shape=(pl...  62.2 us
    pallas_call x1, Pallas kernels, on_device(): pl.pallas_call(write_back, out_shape=(jax.ShapeDtypeStruct((3, nx, ny, nz...  4.73 us

profile of v4, /device:TPU:0, one launch (start us, length us, event | category | flops | bytes accessed | tf_op | source)
XLA Modules:
  0.0 68.2 jit_solution(11323385466688259961)
XLA Ops:
  1.3 62.2 %shard_map.103 = (f32[3,16,64,768]{3,2,1,0:T(8,128)S(1)}, f32[16,64,768]{2,1,0:T(8,128)S(1)}, f32[2,64]{1,0:T(2,128)S(1)}) custom-call(f32[3,16,64,768]{3,2,1,0:T(8,128)} %vel.1, f32[16,64,768]{2,1,0:T(8,128)} %pre.1, s32[1,512]{1,0:T(1,128)} %cell_h.1, s32[1,512]{1,0:T(1,128)} %bitcast.1, s32[1,512]{1,0:T(1,128)} %section_h.1, f32[2,64,256]{2,1,0:T(8,128)} %polar.1, ...), custom_call_target="tpu_custom_call" | custom-call | tf_op jit(solution)/shard_map/pallas_call | solution.py:759
  63.5 4.7 %shard_map.104 = (f32[3,16,64,768]{3,2,1,0:T(8,128)}, f32[16,64,768]{2,1,0:T(8,128)}, f32[2,64]{1,0:T(2,128)}) custom-call(f32[3,16,64,768]{3,2,1,0:T(8,128)S(1)} %get-tuple-element.6.fields, f32[16,64,768]{2,1,0:T(8,128)S(1)} %get-tuple-element.7.settled, f32[2,64]{1,0:T(2,128)S(1)} %get-tuple-element.8.loads), custom_call_target="tpu_custom_call" | custom-call | tf_op jit(solution)/shard_map/pallas_call | solution.py:823
